TPU v7x, 256 devices: a whole 4x4x8 slice. The times are simulated.
256 devices in a mesh: pipe: 2 (over z_lo), rep: 4 (over z_hi), shard: 32 (over y, x, core).
Axes of the slice: x: 4, y: 4, z: 8 (z_hi: 4, z_lo: 2; z = z_hi * 2 + z_lo), core: 2. Of those that a mesh axis runs over, the one named last changes fastest.
Arguments:
- hidden_in: bfloat16 [2, 16384, 8192], P('pipe', ('rep', 'shard')), may hold values from -600 to 600
- query_rows: bfloat16 [2, 16384, 4096], P('pipe', ('rep', 'shard')), may hold values from -160 to 160
- key_rows: bfloat16 [2, 16384, 512], P('pipe', ('rep', 'shard')), may hold values from -6 to 6
- context_grad: bfloat16 [2, 16384, 4096], P('pipe', ('rep', 'shard')), may hold values from -6 to 6
- stream_top: bfloat16 [16384, 8192], P(('rep', 'shard')), may hold values from -4 to 4
- norm_gain: float32 [2, 8192], P('pipe'), may hold values from 0.1 to 1.9
- value_weight: bfloat16 [2, 8192, 512], P('pipe', 'shard'), may hold values from -0.0625 to 0.0625
Outputs:
- stream_grad: bfloat16 [2, 16384, 8192], P('pipe', ('rep', 'shard'))
- query_grad: bfloat16 [2, 16384, 4096], P('pipe', ('rep', 'shard'))
- key_grad: bfloat16 [2, 16384, 512], P('pipe', ('rep', 'shard'))
- value_weight_grad: float32 [2, 8192, 512], P('pipe', 'shard')
- gain_grad: float32 [2, 8192], P('pipe', 'shard')
All inputs are finite; a program needn't handle non-finite values.
Results may differ from a plain program's by a relative error of at most 0.025.
Values may be sent and summed in bfloat16 or wider, within the bound.
A program may use at most 128 MiB of HBM per device.

v0:
```python
import jax
import jax.numpy as jnp
from jax import lax
from jax.sharding import PartitionSpec as P

HEAD_DIM = 128
QHEADS = 32
KVHEADS = 4


EPSILON = 1e-05


def from_behind(x, axis, by):
    peers = lax.axis_size(axis)
    pairs = [(i, i + by) for i in range(peers) if 0 <= i + by < peers]
    return lax.ppermute(x, axis, pairs)


def attend_back(query_rows, key_rows, values, context_grad):
    row_count = query_rows.shape[0]
    groups = QHEADS // KVHEADS
    score_scale = 1.0 / HEAD_DIM**0.5
    query_heads = query_rows.reshape(row_count, KVHEADS, groups, HEAD_DIM)
    key_heads = key_rows.reshape(row_count, KVHEADS, HEAD_DIM)
    value_heads = values.reshape(row_count, KVHEADS, HEAD_DIM)
    grad_heads = context_grad.reshape(row_count, KVHEADS, groups, HEAD_DIM)
    scores = (
        jnp.einsum("tkgd,ukd->kgtu", query_heads, key_heads, preferred_element_type=jnp.float32)
        * score_scale
    )
    positions = jnp.arange(row_count)
    allowed = positions[None, :] <= positions[:, None]
    scores = jnp.where(allowed, scores, -1e30)
    top_score = jnp.max(scores, axis=-1, keepdims=True)
    weights_raw = jnp.exp(scores - top_score)
    probs = weights_raw / jnp.sum(weights_raw, axis=-1, keepdims=True)
    probs_low = probs.astype(jnp.bfloat16)
    grad_prob = jnp.einsum(
        "tkgd,ukd->kgtu", grad_heads, value_heads, preferred_element_type=jnp.float32
    )
    row_dot = jnp.sum(probs * grad_prob, axis=-1, keepdims=True)
    grad_score = (probs * (grad_prob - row_dot) * score_scale).astype(jnp.bfloat16)
    query_grad = jnp.einsum(
        "kgtu,ukd->tkgd", grad_score, key_heads, preferred_element_type=jnp.float32
    )
    key_grad = jnp.einsum(
        "kgtu,tkgd->ukd", grad_score, query_heads, preferred_element_type=jnp.float32
    )
    value_grad = jnp.einsum(
        "kgtu,tkgd->ukd", probs_low, grad_heads, preferred_element_type=jnp.float32
    )
    return (
        query_grad.reshape(row_count, -1).astype(jnp.bfloat16),
        key_grad.reshape(row_count, -1).astype(jnp.bfloat16),
        value_grad.reshape(row_count, -1).astype(jnp.bfloat16),
    )


def per_device(hidden_in, query_rows, key_rows, context_grad, stream_top, norm_gain, value_weight):
    section_index = lax.axis_index("pipe")
    top_section = lax.axis_size("pipe") - 1
    hidden_wide = hidden_in[0].astype(jnp.float32)
    gain_row = norm_gain[0]
    inv_rms = lax.rsqrt(jnp.mean(hidden_wide * hidden_wide, axis=-1, keepdims=True) + EPSILON)
    normalized = hidden_wide * inv_rms
    normed = (normalized * gain_row).astype(jnp.bfloat16)
    weight = lax.all_gather(value_weight[0], "shard", axis=0, tiled=True)
    values = jnp.dot(normed, weight, preferred_element_type=jnp.float32).astype(jnp.bfloat16)
    query_grad, key_grad, value_grad = attend_back(
        query_rows[0], key_rows[0], values, context_grad[0]
    )
    normed_grad = lax.dot_general(
        value_grad, weight, (((1,), (1,)), ((), ())), preferred_element_type=jnp.float32
    )
    gain_scaled = normed_grad * gain_row
    branch_grad = inv_rms * (
        gain_scaled - normalized * jnp.mean(gain_scaled * normalized, axis=-1, keepdims=True)
    )
    upper_grad = (stream_top.astype(jnp.float32) + branch_grad).astype(jnp.bfloat16)
    passed = from_behind(upper_grad, "pipe", -1)
    lower_grad = (passed.astype(jnp.float32) + branch_grad).astype(jnp.bfloat16)
    stream = jnp.where(section_index == top_section, upper_grad, lower_grad)
    shard_count = lax.axis_size("shard")
    rep_count = lax.axis_size("rep")
    row_count = hidden_in.shape[1]
    grad_scale = float(row_count * shard_count * rep_count) ** (-0.5)
    gain_term = jnp.sum(normed_grad * normalized, axis=0)
    weight_term = lax.dot_general(
        normed, value_grad, (((0,), (0,)), ((), ())), preferred_element_type=jnp.float32
    )
    weight_part, gain_part = (
        lax.psum_scatter(
            weight_term.astype(jnp.bfloat16), "shard", scatter_dimension=0, tiled=True
        ).astype(jnp.float32),
        lax.psum_scatter(
            gain_term.astype(jnp.bfloat16), "shard", scatter_dimension=0, tiled=True
        ).astype(jnp.float32),
    )
    weight_total, gain_total = (
        lax.psum(weight_part.astype(jnp.bfloat16), "rep").astype(jnp.float32),
        lax.psum(gain_part.astype(jnp.bfloat16), "rep").astype(jnp.float32),
    )
    return (
        stream[None],
        query_grad[None],
        key_grad[None],
        (weight_total * grad_scale)[None],
        (gain_total * grad_scale)[None],
    )


def solution(mesh):
    return jax.shard_map(
        per_device,
        mesh=mesh,
        in_specs=(
            P("pipe", ("rep", "shard"), None),
            P("pipe", ("rep", "shard"), None),
            P("pipe", ("rep", "shard"), None),
            P("pipe", ("rep", "shard"), None),
            P(("rep", "shard"), None),
            P("pipe", None),
            P("pipe", "shard", None),
        ),
        out_specs=(
            P("pipe", ("rep", "shard"), None),
            P("pipe", ("rep", "shard"), None),
            P("pipe", ("rep", "shard"), None),
            P("pipe", "shard", None),
            P("pipe", "shard"),
        ),
        check_vma=False,
    )
```

profile of v0, /device:TPU:32, one launch (start us, length us, event | category | flops | bytes accessed | tf_op | source)
XLA Modules:
  0.0 414.5 jit_solution(13965182926582226464)
XLA Ops:
  7.2 0.0 copy-start.8
  7.2 0.0 copy-start.3
  7.2 0.0 reduce-scatter.2.cloned.1.call-start
  7.3 0.0 copy-start.4
  7.3 2.2 fusion.17
  9.5 0.0 copy-done.8
  9.6 0.1 copy.41
  9.7 0.0 copy-done.3
  9.7 1.3 copy.50
  11.0 0.0 copy-done.4
  11.0 0.2 copy.51
  11.3 1.0 copy-done.5
  12.3 2.2 fusion.57
  14.4 2.4 fusion.33
  16.8 0.0 copy-done
  16.8 0.0 copy-done.7
  16.8 5.7 %convolution_convert_fusion = bf16[8192,512]{1,0:T(8,128)(2,1)} fusion(bf16[128,512]{0,1:T(8,128)(2,1)S(1)} %bitcast.126, bf16[1,128,8192]{2,1,0:T(8,128)(2,1)S(1)} %copy-done, f32[8192]{0:T(1024)S(1)} %bitcast.121, f32[128]{0:T(128)S(1)} %add_rsqrt_fusion), kind=kOutput, calls=%fused_computation.2 | convolution fusion | flops 1082130432 | bytes 10650112 | tf_op jit(solution)/shard_map/dot_general | solution.py:89
  22.5 0.0 reduce-scatter.2.cloned.1.call-update
  22.5 0.0 all-gather.3.cloned.1.call-start
  22.6 0.7 all-gather.3.cloned.1.call-update
  23.3 0.0 all-reduce.3.cloned.1.call-start
  23.3 102.2 %reduce-scatter.2.cloned.1.call-done = bf16[256,512]{1,0:T(8,128)(2,1)} async-done(((bf16[8192,512]{1,0:T(8,128)(2,1)}), bf16[256,512]{1,0:T(8,128)(2,1)}) %reduce-scatter.2.cloned.1.call-update) | async-done | bytes 262160 | tf_op jit(solution)/shard_map/reduce_scatter | solution.py:93
  125.5 0.0 all-reduce.3.cloned.1.call-update
  125.6 60.2 %all-gather.3.cloned.1.call-done = bf16[1,8192,512]{2,1,0:T(8,128)(2,1)} async-done(((bf16[1,256,512]{2,1,0:T(8,128)(2,1)}), bf16[1,8192,512]{2,1,0:T(8,128)(2,1)}) %all-gather.3.cloned.1.call-update) | async-done | bytes 8388624 | tf_op jit(solution)/shard_map/all_gather | solution.py:68
  185.8 7.0 %fusion.16 = (bf16[8192]{0:T(1024)(128)(2,1)S(1)}, f32[128]{0:T(128)S(1)}, f32[128,8192]{1,0:T(8,128)S(1)}) fusion(bf16[1,128,8192]{2,1,0:T(8,128)(2,1)S(1)} %copy-done, f32[128]{0:T(128)S(1)} %add_rsqrt_fusion, f32[8192]{0:T(1024)S(1)} %bitcast.122, bf16[128,512]{0,1:T(8,128)(2,1)S(1)} %bitcast.127, bf16[1,8192,512]{2,1,0:T(8,128)(2,1)} %all-gather.3.cloned.1.call-done), kind=kOutput, calls=%fused_computation.19 | convolution fusion | flops 1081073536 | bytes 14861312 | tf_op jit(solution)/shard_map/dot_general | solution.py:73
  192.8 0.0 copy-start.1
  192.8 0.0 copy-done.2
  192.8 0.0 copy-start.9
  192.8 2.7 add_convert_fusion.1
  195.5 0.0 copy-done.1
  195.5 3.7 collective-permute-start
  199.3 0.0 copy-done.9
  199.3 0.6 dynamic-slice
  200.5 38.8 %all-reduce.3.cloned.1.call-done = bf16[256,512]{1,0:T(8,128)(2,1)} async-done(((bf16[256,512]{1,0:T(8,128)(2,1)}), bf16[256,512]{1,0:T(8,128)(2,1)}) %all-reduce.3.cloned.1.call-update) | async-done | bytes 262160 | tf_op jit(solution)/shard_map/psum | solution.py:101
  239.4 1.8 multiply_bitcast_fusion
  241.2 5.3 %fusion.35 = bf16[128,512]{1,0:T(8,128)(2,1)} fusion(bf16[1,8192,512]{2,1,0:T(8,128)(2,1)} %all-gather.3.cloned.1.call-done, bf16[1,128,8192]{2,1,0:T(8,128)(2,1)S(1)} %copy-done, f32[8192]{0:T(1024)S(1)} %bitcast.124, f32[128]{0:T(128)S(1)} %add_rsqrt_fusion), kind=kOutput, calls=%fused_computation.45 | convolution fusion | flops 1078001664 | bytes 10650112 | tf_op jit(solution)/shard_map/dot_general | solution.py:69
  246.5 0.9 reshape.71
  247.4 1.9 fusion.46
  249.3 5.4 %convolution_convert_fusion.1 = bf16[4,8,128,128]{2,3,1,0:T(8,128)(2,1)} fusion(bf16[128,4,128,1]{0,2,3,1:T(8,128)(2,1)S(1)} %copy.41, f32[4,128,128,8]{2,1,3,0:T(8,128)} %fusion.46, f32[4,8,128,128]{2,3,1,0:T(8,128)} %get-tuple-element.18, f32[4,8,128]{2,1,0:T(8,128)S(1)} %get-tuple-element.17), kind=kOutput, calls=%fused_computation.40 | convolution fusion | flops 138416256 | bytes 5390336 | tf_op jit(solution)/shard_map/kgtu,ukd->tkgd/dot_general | solution.py:44
  254.7 2.4 copy.34
  257.1 4.3 %fusion.34 = bf16[4,128,128]{1,2,0:T(8,128)(2,1)S(1)} fusion(bf16[128,4,8,128]{0,3,2,1:T(8,128)(2,1)S(1)} %bitcast.117, f32[4,128,128,8]{2,1,3,0:T(8,128)} %fusion.46, f32[4,8,128,128]{2,3,1,0:T(8,128)} %get-tuple-element.18, f32[4,8,128]{2,1,0:T(8,128)S(1)} %get-tuple-element.17), kind=kOutput, calls=%fused_computation.44 | convolution fusion | flops 137957504 | bytes 5390336 | tf_op jit(solution)/shard_map/kgtu,tkgd->ukd/dot_general | solution.py:47
  261.4 0.8 copy.35
  262.2 126.9 %all-reduce = bf16[8192]{0:T(1024)(128)(2,1)S(1)} all-reduce(bf16[8192]{0:T(1024)(128)(2,1)S(1)} %get-tuple-element.15), channel_id=4, replica_groups=mesh['pipe'=2,'rep'=4,'shard'=32] {'shard'}, use_global_device_ids=true, to_apply=%region_8.9.clone | all-reduce | flops 8192 | bytes 32768
  389.1 0.1 dynamic-slice.1
  389.2 11.7 %psum.15 = bf16[256]{0:T(256)(128)(2,1)S(1)} all-reduce(bf16[256]{0:T(256)(128)(2,1)S(1)} %dynamic-slice.1), channel_id=1, replica_groups=mesh['pipe'=2,'rep'=4,'shard'=32] {'rep'}, use_global_device_ids=true, to_apply=%region_9.10 | all-reduce | flops 256 | bytes 1024 | tf_op jit(solution)/shard_map/psum | solution.py:102
  400.9 0.6 convert_multiply_fusion.1
  401.5 0.0 collective-permute-done
  401.5 6.5 %fusion.21 = bf16[1,128,8192]{2,1,0:T(8,128)(2,1)} fusion(bf16[128,8192]{1,0:T(8,128)(2,1)} %collective-permute-done, pred[]{:T(512)S(6)} %eq.3, f32[128]{0:T(128)S(1)} %broadcast_multiply_fusion, bf16[1,128,8192]{2,1,0:T(8,128)(2,1)S(1)} %copy-done, f32[128,8192]{1,0:T(8,128)} %copy-done.1, f32[8192]{0:T(1024)S(1)} %bitcast.125, f32[128]{0:T(128)S(1)} %add_rsqrt_fusion, ...), kind=kLoop, calls=%fused_computation.26 | loop fusion | flops 13631488 | bytes 12616705 | tf_op jit(solution)/shard_map/broadcast_in_dim | solution.py:105
  (10 shorter events, 0.1 us)
Async XLA Ops:
  7.2 2.3 copy-start.8
  7.2 2.5 copy-start.3
  7.2 118.4 %reduce-scatter.2.cloned.1.call-start = ((), (), s32[]{:S(2)}) async-start(), calls=%async_computation.1 | async-start | bytes 8650752 | tf_op jit(solution)/shard_map/reduce_scatter | solution.py:93
  7.3 3.8 copy-start.4
  11.0 1.2 copy-start.5
  14.4 2.4 copy-start
  14.4 2.4 copy-start.7
  22.5 163.3 %all-gather.3.cloned.1.call-start = ((), (), s32[]{:S(2)}) async-start(), calls=%async_computation.3 | async-start | bytes 8650752 | tf_op jit(solution)/shard_map/all_gather | solution.py:68
  23.3 216.1 %all-reduce.3.cloned.1.call-start = ((), (), s32[]{:S(2)}) async-start(), calls=%async_computation.2 | async-start | bytes 524288 | tf_op jit(solution)/shard_map/psum | solution.py:101
  185.8 7.0 %copy-start.2 = (bf16[128,8192]{1,0:T(8,128)(2,1)S(1)}, bf16[128,8192]{1,0:T(8,128)(2,1)}, u32[]{:S(2)}) copy-start(bf16[128,8192]{1,0:T(8,128)(2,1)} %param.11) | copy-start | bytes 6291460
  192.8 2.8 copy-start.1
  192.8 6.5 %copy-start.9 = (u32[256]{0:T(256)S(1)}, u32[256]{0:T(256)}, u32[]{:S(2)}) copy-start(u32[256]{0:T(256)} %constant.33) | copy-start | bytes 3076
  195.5 205.9 %collective-permute-start = (bf16[128,8192]{1,0:T(8,128)(2,1)}, bf16[128,8192]{1,0:T(8,128)(2,1)}, u32[]{:S(2)}, u32[]{:S(2)}) collective-permute-start(bf16[128,8192]{1,0:T(8,128)(2,1)} %add_convert_fusion.1), channel_id=1, source_target_pairs={{128,0},{129,1},{130,2},{131,3},{132,4},{133,5},{134,6},{135,7},{1... | collective-permute-start | bytes 6291464 | tf_op jit(solution)/shard_map/ppermute | solution.py:17
  254.7 2.4 copy-start.6
Sparse Core Ops, SparseCore 0:
  22.6 102.8 reduce-scatter.1
  128.4 57.3 all-gather.2
  188.6 50.6 all-reduce.2
where the time goes:
time: 415 us
  waiting for transfers between devices  202 us (49%)
  blocking collectives  139 us (33%)
  matrix products  34.1 us (8%)
  between operations  14.5 us (3%)
  other arithmetic  13.8 us (3%)
  local copies, waits for them, and re-layouts  7.47 us (2%)
    unnamed x1, blocking collectives  127 us
    reduce_scatter x1, waiting for transfers between devices, per_device(): lax.psum_scatter(weight_term.astype(jnp.bfloat16), 'shard', scatter_dimen...  102 us
    all_gather x1, waiting for transfers between devices, per_device(): weight = lax.all_gather(value_weight[0], 'shard', axis=0, tiled=True)  60.2 us
    psum x1, waiting for transfers between devices, per_device(): lax.psum(weight_part.astype(jnp.bfloat16), 'rep').astype(jnp.float32)  38.8 us
    psum x1, blocking collectives, per_device(): lax.psum(gain_part.astype(jnp.bfloat16), 'rep').astype(jnp.float32)  11.7 us
  transfers between devices with their start and end apart: 4, of which 3 were waited for; matrix products, arithmetic and copies ran while one was open for 8% of the time, Pallas kernels for 0%

commit v1 on v0

v1 whole, which is shorter than its diff:
```python
import itertools

import jax
import jax.numpy as jnp
from jax import lax
from jax.experimental import pallas as pl
from jax.experimental.pallas import tpu as pltpu
from jax.sharding import PartitionSpec as P

D = 8192
HEAD = 128
QHEADS = 32
KV = 4
GROUP = QHEADS // KV
TOK = 128
KVW = KV * HEAD
BLK = 256
EPSILON = 1e-05
SCORE_SCALE = 1.0 / HEAD**0.5
GRAD_SCALE = 16384.0**-0.5
F32, BF16 = jnp.float32, jnp.bfloat16

ORDER = (
    (0, 0), (3, 0), (1, 0), (0, 3), (0, 1), (2, 0), (0, 2),
    (3, 3), (1, 3), (3, 1), (1, 1), (2, 3), (2, 1), (3, 2), (1, 2), (2, 2),
)
EARLY = 7
NSEM = 176


def dot(a, b):
    return jnp.dot(a, b, preferred_element_type=F32)


def dot_nt(a, b):
    return lax.dot_general(a, b, (((1,), (1,)), ((), ())), preferred_element_type=F32)


def kernel(
    hid_h, query_h, key_h, ctx_h, top_h, gain_h, w_h,
    stream_o, qg_o, kg_o, vwg_o, gg_o,
    hid, hsib, query, key, ctx, top, gain, gain1, inv, inv_sib, inv1, cen, cen1,
    w_all, w1, normed, vg, vg1, vgt, probs, vpart, vrecv, values,
    ng, ng_stage, ng1, ng1_stage, hid1, stream, late,
    wt, rbuf, fin, rep_stage, rep_recv, rep_all, wown, qg, kg, vwg, gg,
    ssem, rsem, lsem,
):
    pipe = lax.axis_index("pipe")
    rep = lax.axis_index("rep")
    shard = lax.axis_index("shard")
    core = lax.rem(shard, 2)
    chip = lax.div(shard, 2)
    x, y = lax.rem(chip, 4), lax.div(chip, 4)
    is_top = pipe == 1
    is_low = pipe == 0
    ids = itertools.count()
    local_ids = itertools.count()
    sent = []

    def chip_at(dx, dy):
        return lax.rem(y + dy % 4, 4) * 4 + lax.rem(x + dx % 4, 4)

    def peer(dx, dy):
        return {"shard": chip_at(dx, dy) * 2 + core}

    sibling = {"shard": chip * 2 + (1 - core)}
    below = {"pipe": 0}
    ahead = {"pipe": 0, "rep": lax.rem(rep + 1, 4)}

    def remote(src, dst, device, who=None):
        number = next(ids)
        copy = pltpu.make_async_remote_copy(
            src_ref=src, dst_ref=dst, send_sem=ssem.at[number], recv_sem=rsem.at[number],
            device_id=device, device_id_type=pl.DeviceIdType.MESH,
        )
        sent.append((copy, who))
        return copy

    def send(src, dst, device):
        copy = remote(src, dst, device)
        copy.start()
        return copy

    def local(src, dst):
        copy = pltpu.make_async_copy(src, dst, lsem.at[next(local_ids)])
        copy.start()
        return copy

    def cols(start, width):
        return pl.ds(pl.multiple_of(start, 128), width)

    load_hid = local(hid_h, hid)
    load_gain = local(gain_h, gain)
    load_key = local(key_h, key)
    load_query = local(query_h, query)
    load_ctx = local(ctx_h, ctx)
    load_w = local(w_h, w_all.at[chip])
    load_top = local(top_h, top)

    barrier = pltpu.get_barrier_semaphore()
    partners = [peer(1, 0), peer(3, 0), peer(0, 1), peer(0, 3), sibling, {"pipe": 1 - pipe}]
    partners += [{"rep": lax.rem(rep + o, 4)} for o in (1, 2, 3)]
    partners += [{"pipe": 1 - pipe, "rep": lax.rem(rep + jnp.where(is_top, 1, 3), 4)}]
    for device in partners:
        pl.semaphore_signal(barrier, inc=1, device_id=device, device_id_type=pl.DeviceIdType.MESH)
    pl.semaphore_wait(barrier, len(partners))

    def step(half, first, by):
        along_x = (half == 0) == first
        return (by, 0) if along_x else (0, by)

    def shift(half, first_by, second_by):
        return (first_by, second_by) if half == 0 else (second_by, first_by)

    def rows(half, quarter=None):
        if quarter is None:
            return pl.ds(half * 128, 128)
        return pl.ds(half * 128 + quarter * 64, 64)

    gather = {}

    def gather_own(half, first):
        for kind, by in ((0, 1), (1, 3)):
            src = w_h.at[rows(half), :]
            gather[half, first, 0, kind] = send(
                src, w_all.at[chip, rows(half), :], peer(*step(half, first, by))
            )

    def gather_pass(half, offset, index):
        j = chip_at(*shift(half, offset, 0))
        for kind, by in ((0, 1), (1, 3)):
            part = w_all.at[j, rows(half), :]
            gather[half, False, index, kind] = send(part, part, peer(*step(half, False, by)))

    def gather_forward(half, first, index, offset):
        for kind, by in ((0, 3), (1, 1)):
            gather[half, first, index, kind].wait_recv()
            move = shift(half, by, 0) if first else shift(half, offset, by)
            part = w_all.at[chip_at(*move), rows(half, kind), :]
            to = 1 if kind == 0 else 3
            gather[half, first, index, kind + 2] = send(part, part, peer(*step(half, first, to)))

    def gather_end(half, first, index):
        for kind in (2, 3):
            gather[half, first, index, kind].wait_recv()

    early = []
    for e in range(EARLY):
        j = chip_at(*ORDER[e])
        early.append((
            j,
            remote(hid_h.at[:, cols(j * 512, 512)], hid1.at[:, pl.ds(e * 512, 512)], below, "down"),
            remote(w_h if e == 0 else w_all.at[j], w1.at[e], ahead, "down"),
        ))
    send_gain1 = remote(gain_h, gain1, below, "down")

    for half in (0, 1):
        gather_own(half, True)
    for half in (0, 1):
        gather_own(half, False)
    hsib_copies = []
    for j in range(16):
        hsib_copies.append(send(
            hid_h.at[:, cols((2 * j + 1 - core) * BLK, BLK)], hsib.at[:, pl.ds(j * BLK, BLK)], sibling
        ))

    @pl.when(is_top)
    def _():
        early[0][2].start()
        send_gain1.start()
        for _, down, _ in early:
            down.start()

    load_hid.wait()
    load_gain.wait()

    def square(i, total):
        part = hid[:, cols(i * 512, 512)].astype(F32)
        part = part * part
        for n in range(4):
            total = total + part[:, n * 128:(n + 1) * 128]
        return total

    total = lax.fori_loop(0, 16, square, jnp.zeros((TOK, 128), F32))
    mean = jnp.sum(total, axis=1, keepdims=True) * (1.0 / D)
    inv[...] = jnp.broadcast_to(lax.rsqrt(mean + EPSILON), (TOK, 128))
    send_inv = send(inv, inv_sib, sibling)
    send_inv1 = remote(inv, inv1, below, "down")

    @pl.when(is_top)
    def _():
        send_inv1.start()

    load_key.wait()
    load_query.wait()
    load_ctx.wait()

    def stacked(ref, k):
        return jnp.concatenate(
            [ref[:, (GROUP * k + g) * HEAD:(GROUP * k + g + 1) * HEAD] for g in range(GROUP)], axis=0
        )

    def attend(k):
        lanes = slice(k * HEAD, (k + 1) * HEAD)
        scores = dot_nt(key[:, lanes], stacked(query, k)) * SCORE_SCALE
        u = lax.broadcasted_iota(jnp.int32, scores.shape, 0)
        t = lax.broadcasted_iota(jnp.int32, scores.shape, 1) & (TOK - 1)
        scores = jnp.where(u <= t, scores, -1e30)
        raw = jnp.exp(scores - jnp.max(scores, axis=0, keepdims=True))
        prob = raw / jnp.sum(raw, axis=0, keepdims=True)
        probs[k] = prob
        vg[0:TOK, lanes] = dot(prob.astype(BF16), stacked(ctx, k)).astype(BF16)

    attend(0)
    for half in (0, 1):
        gather_forward(half, True, 0, 0)
        gather_pass(half, 3, 1)
        gather_pass(half, 1, 2)
    attend(1)
    for half in (0, 1):
        gather_forward(half, False, 0, 0)
    load_w.wait()

    @pl.when(is_top)
    def _():
        for e in range(1, 5):
            early[e][2].start()

    attend(2)
    for half in (0, 1):
        gather_end(half, True, 0)
        gather_pass(half, 2, 3)
    attend(3)

    send_vg = send(vg.at[pl.ds(0, TOK), :], vg.at[pl.ds(TOK, TOK), :], sibling)
    send_vg1 = remote(vg.at[pl.ds(0, TOK), :], vg1.at[pl.ds(0, TOK), :], below, "down")

    @pl.when(is_top)
    def _():
        send_vg1.start()

    for half in (0, 1):
        gather_end(half, False, 0)

    @pl.when(is_top)
    def _():
        for e in range(5, 7):
            early[e][2].start()

    for copy in hsib_copies:
        copy.wait_recv()
    send_inv.wait_recv()

    def norm_block(j, carry):
        gain_row = gain[:, cols((2 * j + core) * BLK, BLK)]
        own = hid[:, cols((2 * j + core) * BLK, BLK)].astype(F32) * inv[:, 0:1]
        other = hsib[:, cols(j * BLK, BLK)].astype(F32) * inv_sib[:, 0:1]
        normed[0:TOK, cols(j * BLK, BLK)] = (own * gain_row).astype(BF16)
        normed[TOK:, cols(j * BLK, BLK)] = (other * gain_row).astype(BF16)
        return carry

    lax.fori_loop(0, 16, norm_block, 0)
    for half in (0, 1):
        gather_forward(half, False, 1, 3)
        gather_forward(half, False, 2, 1)

    send_vg.wait_recv()
    vgt[...] = vg[...].astype(F32).T.astype(BF16)

    def weight_block(j, carry):
        wt[j] = dot(vgt[...], normed[:, cols(j * BLK, BLK)]).astype(BF16)
        return carry

    ng_copies = []

    def value_block(place):
        j = chip_at(*ORDER[place])
        block = w_all[j]
        part = dot(normed[:, cols(j * BLK, BLK)], block)
        if place == 0:
            vpart[...] = part
        else:
            vpart[...] += part
        grad = dot_nt(vg[...], block)
        where = cols((2 * j + core) * BLK, BLK)
        ng[:, where] = grad[0:TOK].astype(BF16)
        ng_stage[place] = grad[TOK:].astype(BF16)
        ng_copies.append(send(ng_stage.at[place], ng.at[:, where], sibling))

    for place in range(0, 4):
        value_block(place)
    for half in (0, 1):
        gather_forward(half, False, 3, 2)
    for place in range(4, 11):
        value_block(place)
    for half in (0, 1):
        gather_end(half, False, 1)
        gather_end(half, False, 2)
    for place in range(11, 15):
        value_block(place)
    lax.fori_loop(0, 16, weight_block, 0)
    for half in (0, 1):
        gather_end(half, False, 3)
    value_block(15)
    send_part = send(vpart.at[pl.ds(TOK, TOK), :], vrecv, sibling)

    def wrows(half, quarter):
        return pl.ds(half * 256 + quarter * 128, 128)

    scatter = {}

    def place_of(half, line, by):
        move = shift(half, by, line) if line < 4 else shift(half, 0, by)
        return chip_at(*move)

    def scatter_send(half, line, kind, by, quarter, to):
        scatter[half, line, kind] = send(
            wt.at[place_of(half, line, by), wrows(half, quarter), :],
            rbuf.at[half * 5 + line, kind],
            peer(*step(half, line < 4, to)),
        )

    def scatter_far(half, line):
        scatter_send(half, line, 0, 2, 0, 1)
        scatter_send(half, line, 1, 2, 1, 3)

    def scatter_near(half, line):
        scatter_send(half, line, 2, 1, 1, 1)
        scatter_send(half, line, 3, 3, 0, 3)

    def add_in(half, line, by, quarter, kinds):
        j = place_of(half, line, by)
        total = wt[j, wrows(half, quarter), :].astype(F32)
        for kind in kinds:
            total = total + rbuf[half * 5 + line, kind].astype(F32)
        return j, total

    def scatter_forward(half, line):
        for kind, by, quarter in ((0, 1, 0), (1, 3, 1)):
            scatter[half, line, kind].wait_recv()
            j, total = add_in(half, line, by, quarter, (kind,))
            wt[j, wrows(half, quarter), :] = total.astype(BF16)
            scatter_send(half, line, kind + 4, by, quarter, by)

    def scatter_own(half, line):
        for kind in (2, 3, 4, 5):
            scatter[half, line, kind].wait_recv()
        for quarter, kinds in ((0, (3, 4)), (1, (2, 5))):
            j, total = add_in(half, line, 0, quarter, kinds)
            if line < 4:
                wt[j, wrows(half, quarter), :] = total.astype(BF16)
            else:
                fin[wrows(half, quarter), :] = total

    lines = (2, 1, 3, 0)
    for line in lines:
        for half in (0, 1):
            scatter_far(half, line)
    for line in lines:
        for half in (0, 1):
            scatter_near(half, line)

    send_part.wait_recv()
    whole = vpart[0:TOK, :] + vrecv[...]
    values[...] = whole.astype(BF16)
    mean = jnp.sum(whole * vg[0:TOK, :].astype(F32), axis=1, keepdims=True) * (1.0 / D)
    cen[...] = jnp.broadcast_to(mean, (TOK, 128))
    send_cen1 = remote(cen, cen1, below, "down")

    for copy in ng_copies:
        copy.wait_recv()
    load_top.wait()

    def branch(hidden, scale, grad, gain_row, center):
        factor = scale[:, 0:1]
        normalized = hidden.astype(F32) * factor
        return factor * (grad.astype(F32) * gain_row - normalized * center[:, 0:1])

    def own_branch(where):
        return branch(hid[:, where], inv, ng[:, where], gain[:, where], cen)

    lates = []
    for e in range(EARLY, 16):
        j = chip_at(*ORDER[e])
        where = cols(j * 512, 512)
        lates.append((j, remote(
            stream.at[:, where], late.at[:, pl.ds((e - EARLY) * 512, 512)], below, "down"
        )))
    outs = [
        pltpu.make_async_copy(
            stream.at[:, pl.ds(n * 512, 512)], stream_o.at[:, pl.ds(n * 512, 512)], lsem.at[next(local_ids)]
        )
        for n in range(16)
    ]

    def top_block(j):
        where = cols(j * 512, 512)
        stream[:, where] = (top[:, where].astype(F32) + own_branch(where)).astype(BF16)

    @pl.when(is_top)
    def _():
        send_cen1.start()
        for j, copy in lates:
            top_block(j)
            copy.start()

    for half in (0, 1):
        scatter_forward(half, 2)

    def attend_back(k):
        lanes = slice(k * HEAD, (k + 1) * HEAD)
        queries, grads = stacked(query, k), stacked(ctx, k)
        prob = probs[k]
        grad_prob = dot_nt(values[:, lanes], grads)
        row_dot = jnp.sum(prob * grad_prob, axis=0, keepdims=True)
        wide = prob * (grad_prob - row_dot) * SCORE_SCALE
        grad_score = wide.astype(BF16)
        kg[:, lanes] = dot(grad_score, queries).astype(BF16)
        for g in range(GROUP):
            turned = wide[:, g * HEAD:(g + 1) * HEAD].T.astype(BF16)
            head = (GROUP * k + g) * HEAD
            qg[:, head:head + HEAD] = dot(turned, key[:, lanes]).astype(BF16)

    attend_back(0)
    for line in (1, 3):
        for half in (0, 1):
            scatter_forward(half, line)
    attend_back(1)
    for half in (0, 1):
        scatter_forward(half, 0)
        scatter_own(half, 2)
        scatter_far(half, 4)
    attend_back(2)
    for half in (0, 1):
        scatter_own(half, 1)
        scatter_own(half, 3)
        scatter_near(half, 4)
    attend_back(3)
    out_qg = local(qg, qg_o)
    out_kg = local(kg, kg_o)
    for half in (0, 1):
        scatter_own(half, 0)
        scatter_forward(half, 4)

    ng1_copies = []
    forward_vg1 = remote(vg1.at[pl.ds(0, TOK), :], vg1.at[pl.ds(TOK, TOK), :], sibling, "low")
    for e in range(EARLY):
        where = cols(e * 512 + core * BLK, BLK)
        ng1_copies.append(remote(ng1_stage.at[e], ng1.at[:, where], sibling, "low"))

    @pl.when(is_low)
    def _():
        send_vg1.wait_recv()
        forward_vg1.start()
        forward_vg1.wait_recv()
        for e in range(EARLY):
            early[e][2].wait_recv()
            grad = dot_nt(vg1[...], w1[e])
            ng1[:, cols(e * 512 + core * BLK, BLK)] = grad[0:TOK].astype(BF16)
            ng1_stage[e] = grad[TOK:].astype(BF16)
            ng1_copies[e].start()
        send_inv1.wait_recv()
        send_gain1.wait_recv()
        send_cen1.wait_recv()
        for e in range(EARLY):
            ng1_copies[e].wait_recv()
            early[e][1].wait_recv()
            here = pl.ds(e * 512, 512)
            where = cols(early[e][0] * 512, 512)
            upper = branch(hid1[:, here], inv1, ng1[:, here], gain1[:, where], cen1)
            upper = (top[:, where].astype(F32) + upper).astype(BF16)
            stream[:, where] = (upper.astype(F32) + own_branch(where)).astype(BF16)

    @pl.when(is_top)
    def _():
        for j, _, _ in early:
            top_block(j)

    for half in (0, 1):
        scatter_own(half, 4)

    for o in (1, 2, 3):
        q = lax.rem(rep + o, 4)
        rep_stage[o] = fin[pl.ds(pl.multiple_of(q * 128, 128), 128), :].astype(BF16)
    rep_copies = [
        send(rep_stage.at[o], rep_recv.at[o - 1], {"rep": lax.rem(rep + o, 4)}) for o in (1, 2, 3)
    ]
    mine = pl.ds(pl.multiple_of(rep * 128, 128), 128)
    wown[...] = w_all[chip].astype(F32).T
    total = fin[mine, :]
    for o in (1, 2, 3):
        rep_copies[o - 1].wait_recv()
        total = total + rep_recv[o - 1].astype(F32)
    rep_all[rep] = total.astype(BF16)
    all_copies = [
        send(rep_all.at[rep], rep_all.at[rep], {"rep": lax.rem(rep + o, 4)}) for o in (1, 2, 3)
    ]

    @pl.when(is_low)
    def _():
        for e, (j, copy) in enumerate(lates):
            copy.wait_recv()
            where = cols(j * 512, 512)
            upper = late[:, pl.ds(e * 512, 512)].astype(F32)
            stream[:, where] = (upper + own_branch(where)).astype(BF16)

    for copy in outs:
        copy.start()
    for copy in all_copies:
        copy.wait_recv()
    summed = jnp.concatenate([rep_all[q].astype(F32) for q in range(4)], axis=0) * GRAD_SCALE
    vwg[...] = summed.T
    gain_own = gain[:, cols(shard * BLK, BLK)]
    gg[...] = jnp.sum(summed * wown[...], axis=0, keepdims=True) / gain_own
    ends = [local(vwg, vwg_o), local(gg, gg_o), out_qg, out_kg] + outs
    for copy in ends:
        copy.wait()

    for copy, who in sent:
        if who is None:
            copy.wait_send()

    @pl.when(is_top)
    def _():
        for copy, who in sent:
            if who == "down":
                copy.wait_send()

    @pl.when(is_low)
    def _():
        for copy, who in sent:
            if who == "low":
                copy.wait_send()


def per_device(hidden_in, query_rows, key_rows, context_grad, stream_top, norm_gain, value_weight):
    def vmem(*shape, dtype=BF16):
        return pltpu.VMEM(shape, dtype)

    scratch = [
        vmem(TOK, D), vmem(TOK, D // 2), vmem(TOK, 4096), vmem(TOK, KVW), vmem(TOK, 4096), vmem(TOK, D),
        vmem(1, D, dtype=F32), vmem(1, D, dtype=F32),
        *[vmem(TOK, 128, dtype=F32) for _ in range(5)],
        vmem(16, BLK, KVW), vmem(EARLY, BLK, KVW), vmem(2 * TOK, 4096),
        vmem(2 * TOK, KVW), vmem(2 * TOK, KVW), vmem(KVW, 2 * TOK),
        vmem(KV, TOK, GROUP * TOK, dtype=F32),
        vmem(2 * TOK, KVW, dtype=F32), vmem(TOK, KVW, dtype=F32), vmem(TOK, KVW),
        vmem(TOK, D), vmem(16, TOK, BLK), vmem(TOK, EARLY * 512), vmem(EARLY, TOK, BLK),
        vmem(TOK, EARLY * 512), vmem(TOK, D), vmem(TOK, (16 - EARLY) * 512),
        vmem(16, KVW, BLK), vmem(10, 6, 128, BLK), vmem(KVW, BLK, dtype=F32),
        vmem(4, 128, BLK), vmem(3, 128, BLK), vmem(4, 128, BLK), vmem(KVW, BLK, dtype=F32),
        vmem(TOK, 4096), vmem(TOK, KVW), vmem(BLK, KVW, dtype=F32), vmem(1, BLK, dtype=F32),
        pltpu.SemaphoreType.DMA((NSEM,)), pltpu.SemaphoreType.DMA((NSEM,)), pltpu.SemaphoreType.DMA((32,)),
    ]
    outs = pl.pallas_call(
        kernel,
        out_shape=(
            jax.ShapeDtypeStruct((TOK, D), BF16),
            jax.ShapeDtypeStruct((TOK, 4096), BF16),
            jax.ShapeDtypeStruct((TOK, KVW), BF16),
            jax.ShapeDtypeStruct((BLK, KVW), F32),
            jax.ShapeDtypeStruct((1, BLK), F32),
        ),
        in_specs=[pl.BlockSpec(memory_space=pl.ANY)] * 7,
        out_specs=[pl.BlockSpec(memory_space=pl.ANY)] * 5,
        scratch_shapes=scratch,
        compiler_params=pltpu.CompilerParams(
            collective_id=0, has_side_effects=True, vmem_limit_bytes=56 * 1024 * 1024
        ),
        cost_estimate=pl.CostEstimate(flops=5 * 10**9, bytes_accessed=12 * 10**6, transcendentals=10**6),
    )(hidden_in[0], query_rows[0], key_rows[0], context_grad[0], stream_top, norm_gain, value_weight[0])
    stream, query_grad, key_grad, weight_grad, gain_grad = outs
    return stream[None], query_grad[None], key_grad[None], weight_grad[None], gain_grad


def solution(mesh):
    return jax.shard_map(
        per_device,
        mesh=mesh,
        in_specs=(
            P("pipe", ("rep", "shard"), None),
            P("pipe", ("rep", "shard"), None),
            P("pipe", ("rep", "shard"), None),
            P("pipe", ("rep", "shard"), None),
            P(("rep", "shard"), None),
            P("pipe", None),
            P("pipe", "shard", None),
        ),
        out_specs=(
            P("pipe", ("rep", "shard"), None),
            P("pipe", ("rep", "shard"), None),
            P("pipe", ("rep", "shard"), None),
            P("pipe", "shard", None),
            P("pipe", "shard"),
        ),
        check_vma=False,
    )
```

time: 415 us -> 93.5 us (0.23)
  waiting for transfers between devices: 202 us -> 0 us
  blocking collectives: 139 us -> 0 us
  Pallas kernels: 0 us -> 85.9 us
  matrix products: 34.1 us -> 0 us
  between operations: 14.5 us -> 0.66 us
  other arithmetic: 13.8 us -> 0 us
    unnamed x1 -> x0, blocking collectives: 127 us -> none
    reduce_scatter x1 -> x0, waiting for transfers between devices: 102 us -> none  [per_device(): lax.psum_scatter(weight_term.astype(jnp.bfloat16), 'shard', scatter_dimen...]
    pallas_call x0 -> x1, Pallas kernels: none -> 85.9 us  [per_device(): pl.pallas_call(kernel, out_shape=(jax.ShapeDtypeStruct((TOK, D), BF16), j...]
    all_gather x1 -> x0, waiting for transfers between devices: 60.2 us -> none  [per_device(): weight = lax.all_gather(value_weight[0], 'shard', axis=0, tiled=True)]
    psum x1 -> x0, waiting for transfers between devices: 38.8 us -> none  [per_device(): lax.psum(weight_part.astype(jnp.bfloat16), 'rep').astype(jnp.float32)]
    dot_general x7 -> x0, matrix products: 31.9 us -> none  [the longest x1 6.97 us: per_device(): lax.dot_general(value_grad, weight, (((1,), (1,)), ((), ())), preferred_e...]
    psum x1 -> x0, blocking collectives: 11.7 us -> none  [per_device(): lax.psum(gain_part.astype(jnp.bfloat16), 'rep').astype(jnp.float32)]
    broadcast_in_dim x2 -> x0, other arithmetic: 8.3 us -> none  [the longest x1 6.49 us: per_device(): stream[None]]
  transfers between devices with their start and end apart: 4 -> 0, of which waited for: 3 -> 0; matrix products, arithmetic and copies ran while one was open for 8% -> 0% of each run, Pallas kernels for 0% -> 0%
where the time goes in v1:
time: 93.5 us; the launch traced here: 92.7 us
  Pallas kernels  85.9 us (92%)
  local copies, waits for them, and re-layouts  6.2 us (7%)
    pallas_call x1, Pallas kernels, per_device(): pl.pallas_call(kernel, out_shape=(jax.ShapeDtypeStruct((TOK, D), BF16), j...  85.9 us
    unnamed x13, local copies, waits for them, and re-layouts  6.2 us

profile of v1, /device:TPU:32, one launch (start us, length us, event | category | flops | bytes accessed | tf_op | source)
XLA Modules:
  0.0 92.7 jit_solution(11211864766011001504)
XLA Ops:
  0.6 85.9 %shard_map.110 = (bf16[128,8192]{1,0:T(8,128)(2,1)}, bf16[128,4096]{1,0:T(8,128)(2,1)}, bf16[128,512]{1,0:T(8,128)(2,1)}, f32[256,512]{1,0:T(8,128)}, f32[1,256]{1,0:T(1,128)}) custom-call(bf16[128,8192]{1,0:T(8,128)(2,1)} %bitcast.13, bf16[128,4096]{1,0:T(8,128)(2,1)} %bitcast.14, bf16[128,512]{1,0:T(8,128)(2,1)} %bitcast.17, bf16[128,4096]{1,0:T(8,128)(2,1)} %bitcast.15, ...), custom_call_target="tpu_custom_call" | custom-call | flops 5000000000 | bytes 12000000 | tf_op jit(solution)/shard_map/pallas_call | solution.py:555
  86.5 0.0 copy-start
  86.5 3.2 %copy.17 = bf16[1,128,8192]{2,1,0:T(8,128)(2,1)} copy(bf16[1,128,8192]{2,1,0:T(8,128)(2,1)} %bitcast.9) | data formatting | bytes 4194304
  89.7 0.0 copy-done
  89.7 0.0 copy-start.2
  89.7 0.0 copy-start.1
  89.7 0.0 copy-start.3
  89.7 1.0 %copy.18 = bf16[1,128,4096]{2,1,0:T(8,128)(2,1)} copy(bf16[1,128,4096]{2,1,0:T(8,128)(2,1)S(1)} %bitcast.10) | data formatting | bytes 2097152
  90.7 0.0 copy-done.2
  90.7 0.7 copy.19
  91.4 0.0 copy-done.1
  91.4 0.8 copy.20
  92.2 0.0 copy-done.3
  92.2 0.6 copy.21
Async XLA Ops:
  86.5 3.2 %copy-start = (bf16[128,4096]{1,0:T(8,128)(2,1)S(1)}, bf16[128,4096]{1,0:T(8,128)(2,1)}, u32[]{:S(2)}) copy-start(bf16[128,4096]{1,0:T(8,128)(2,1)} %get-tuple-element.11) | copy-start | bytes 3145732
  89.7 1.0 %copy-start.2 = (bf16[128,512]{1,0:T(8,128)(2,1)S(1)}, bf16[128,512]{1,0:T(8,128)(2,1)}, u32[]{:S(2)}) copy-start(bf16[128,512]{1,0:T(8,128)(2,1)} %get-tuple-element.12) | copy-start | bytes 393220
  89.7 1.7 %copy-start.1 = (f32[256,512]{1,0:T(8,128)S(1)}, f32[256,512]{1,0:T(8,128)}, u32[]{:S(2)}) copy-start(f32[256,512]{1,0:T(8,128)} %get-tuple-element.13) | copy-start | bytes 1572868
  89.7 2.4 %copy-start.3 = (f32[1,256]{1,0:T(1,128)S(1)}, f32[1,256]{1,0:T(1,128)}, u32[]{:S(2)}) copy-start(f32[1,256]{1,0:T(1,128)} %get-tuple-element.24) | copy-start | bytes 3076

commit v2 on v1

--- a/solution.py
+++ b/solution.py
@@ -24,8 +24,8 @@
     (0, 0), (3, 0), (1, 0), (0, 3), (0, 1), (2, 0), (0, 2),
     (3, 3), (1, 3), (3, 1), (1, 1), (2, 3), (2, 1), (3, 2), (1, 2), (2, 2),
 )
-EARLY = 7
-NSEM = 176
+EARLY = 8
+NSEM = 228 + 3 * EARLY
 
 
 def dot(a, b):
@@ -38,11 +38,12 @@
 
 def kernel(
     hid_h, query_h, key_h, ctx_h, top_h, gain_h, w_h,
-    stream_o, qg_o, kg_o, vwg_o, gg_o,
+    stream, qg, kg, vwg, gg,
     hid, hsib, query, key, ctx, top, gain, gain1, inv, inv_sib, inv1, cen, cen1,
+    inv_row, inv1_row, cen_row, cen1_row,
     w_all, w1, normed, vg, vg1, vgt, probs, vpart, vrecv, values,
-    ng, ng_stage, ng1, ng1_stage, hid1, stream, late,
-    wt, rbuf, fin, rep_stage, rep_recv, rep_all, wown, qg, kg, vwg, gg,
+    ng, ng_stage, ng1, ng1_stage, hid1, late, own,
+    wt, rbuf, fin, rep_stage, rep_recv, rep_all, wown,
     ssem, rsem, lsem,
 ):
     pipe = lax.axis_index("pipe")
@@ -150,7 +151,10 @@
         early.append((
             j,
             remote(hid_h.at[:, cols(j * 512, 512)], hid1.at[:, pl.ds(e * 512, 512)], below, "down"),
-            remote(w_h if e == 0 else w_all.at[j], w1.at[e], ahead, "down"),
+            [
+                remote((w_h if e == 0 else w_all.at[j]).at[rows(half), :], w1.at[e, rows(half), :], ahead, "down")
+                for half in (0, 1)
+            ],
         ))
     send_gain1 = remote(gain_h, gain1, below, "down")
 
@@ -166,7 +170,8 @@
 
     @pl.when(is_top)
     def _():
-        early[0][2].start()
+        early[0][2][0].start()
+        early[0][2][1].start()
         send_gain1.start()
         for _, down, _ in early:
             down.start()
@@ -185,7 +190,8 @@
     mean = jnp.sum(total, axis=1, keepdims=True) * (1.0 / D)
     inv[...] = jnp.broadcast_to(lax.rsqrt(mean + EPSILON), (TOK, 128))
     send_inv = send(inv, inv_sib, sibling)
-    send_inv1 = remote(inv, inv1, below, "down")
+    inv_row[...] = inv[...].T[0:8, :]
+    send_inv1 = remote(inv_row, inv1_row, below, "down")
 
     @pl.when(is_top)
     def _():
@@ -216,6 +222,12 @@
         gather_forward(half, True, 0, 0)
         gather_pass(half, 3, 1)
         gather_pass(half, 1, 2)
+
+    @pl.when(is_top)
+    def _():
+        for e, half in ((1, 0), (2, 0), (3, 1), (4, 1)):
+            early[e][2][half].start()
+
     attend(1)
     for half in (0, 1):
         gather_forward(half, False, 0, 0)
@@ -223,8 +235,8 @@
 
     @pl.when(is_top)
     def _():
-        for e in range(1, 5):
-            early[e][2].start()
+        for e, half in ((1, 1), (2, 1), (3, 0), (4, 0)):
+            early[e][2][half].start()
 
     attend(2)
     for half in (0, 1):
@@ -245,7 +257,8 @@
     @pl.when(is_top)
     def _():
         for e in range(5, 7):
-            early[e][2].start()
+            for half in (0, 1):
+                early[e][2][half].start()
 
     for copy in hsib_copies:
         copy.wait_recv()
@@ -287,85 +300,161 @@
         ng_stage[place] = grad[TOK:].astype(BF16)
         ng_copies.append(send(ng_stage.at[place], ng.at[:, where], sibling))
 
-    for place in range(0, 4):
+    @pl.when(is_top)
+    def _():
+        for e in range(7, EARLY):
+            for half in (0, 1):
+                early[e][2][half].start()
+
+    def wrows(half, quarter):
+        return pl.ds(half * 256 + quarter * 128, 128)
+
+    scatter = {}
+
+    def place_of(half, line, by):
+        move = shift(half, by, line) if line < 4 else shift(half, 0, by)
+        return chip_at(*move)
+
+    def lanes_of(wave):
+        return pl.ds(wave * 128, 128)
+
+    def scatter_make(wave, half, line, kind, by, quarter, to):
+        scatter[wave, half, line, kind] = remote(
+            wt.at[place_of(half, line, by), wrows(half, quarter), lanes_of(wave)],
+            rbuf.at[wave * 10 + half * 5 + line, kind],
+            peer(*step(half, line < 4, to)),
+        )
+        return scatter[wave, half, line, kind]
+
+    def scatter_send(*what):
+        scatter_make(*what).start()
+
+    def scatter_far(wave, line):
+        for half in (0, 1):
+            scatter_send(wave, half, line, 0, 2, 0, 1)
+            scatter_send(wave, half, line, 1, 2, 1, 3)
+
+    def scatter_near(wave, line):
+        for half in (0, 1):
+            scatter_send(wave, half, line, 2, 1, 1, 1)
+            scatter_send(wave, half, line, 3, 3, 0, 3)
+
+    def add_in(wave, half, line, by, quarter, kinds):
+        j = place_of(half, line, by)
+        total = wt[j, wrows(half, quarter), lanes_of(wave)].astype(F32)
+        for kind in kinds:
+            total = total + rbuf[wave * 10 + half * 5 + line, kind].astype(F32)
+        return j, total
+
+    def scatter_forward(wave, line):
+        for half in (0, 1):
+            for kind, by, quarter in ((0, 1, 0), (1, 3, 1)):
+                scatter[wave, half, line, kind].wait_recv()
+                j, total = add_in(wave, half, line, by, quarter, (kind,))
+                wt[j, wrows(half, quarter), lanes_of(wave)] = total.astype(BF16)
+                scatter_send(wave, half, line, kind + 4, by, quarter, by)
+
+    def scatter_own(wave, line):
+        for half in (0, 1):
+            for kind in (2, 3, 4, 5):
+                scatter[wave, half, line, kind].wait_recv()
+            for quarter, kinds in ((0, (3, 4)), (1, (2, 5))):
+                j, total = add_in(wave, half, line, 0, quarter, kinds)
+                if line < 4:
+                    wt[j, wrows(half, quarter), lanes_of(wave)] = total.astype(BF16)
+                else:
+                    fin[wave, half * 2 + quarter] = total
+
+    rep_copies = {}
+
+    def rep_first(wave):
+        for o in (1, 2, 3):
+            q = lax.rem(rep + o, 4)
+            rep_stage[wave, o] = fin[wave, q].astype(BF16)
+            rep_copies[wave, o] = send(rep_stage.at[wave, o], rep_recv.at[wave, o - 1], {"rep": q})
+
+    def rep_second(wave):
+        total = fin[wave, rep]
+        for o in (1, 2, 3):
+            rep_copies[wave, o].wait_recv()
+            total = total + rep_recv[wave, o - 1].astype(F32)
+        rep_all[wave, rep] = total.astype(BF16)
+        for o in (1, 2, 3):
+            here = rep_all.at[wave, rep]
+            rep_copies[wave, o + 3] = send(here, here, {"rep": lax.rem(rep + o, 4)})
+
+    def scatter_start(wave):
+        for line in (2, 1, 3, 0):
+            scatter_far(wave, line)
+
+    def scatter_start_near(wave):
+        for line in (2, 1, 3, 0):
+            scatter_near(wave, line)
+
+    def scatter_stage(wave, stage):
+        if stage == 0:
+            scatter_forward(wave, 2)
+        elif stage == 1:
+            scatter_forward(wave, 1)
+            scatter_forward(wave, 3)
+        elif stage == 2:
+            scatter_forward(wave, 0)
+            scatter_own(wave, 2)
+            scatter_far(wave, 4)
+        elif stage == 3:
+            scatter_own(wave, 1)
+            scatter_own(wave, 3)
+            scatter_near(wave, 4)
+        elif stage == 4:
+            scatter_own(wave, 0)
+            scatter_forward(wave, 4)
+        elif stage == 5:
+            scatter_own(wave, 4)
+            rep_first(wave)
+        else:
+            rep_second(wave)
+
+    opening = []
+    for line in (2, 1, 3, 0):
+        for half in (0, 1):
+            opening.append(scatter_make(0, half, line, 0, 2, 0, 1))
+            opening.append(scatter_make(0, half, line, 1, 2, 1, 3))
+    for line in (2, 1, 3, 0):
+        for half in (0, 1):
+            opening.append(scatter_make(0, half, line, 2, 1, 1, 1))
+            opening.append(scatter_make(0, half, line, 3, 3, 0, 3))
+
+    def open_scatter():
+        lax.fori_loop(0, 16, weight_block, 0)
+        for copy in opening:
+            copy.start()
+
+    pl.when(is_low)(open_scatter)
+
+    for place in range(0, 7):
         value_block(place)
     for half in (0, 1):
         gather_forward(half, False, 3, 2)
-    for place in range(4, 11):
+    for place in range(7, 11):
         value_block(place)
     for half in (0, 1):
         gather_end(half, False, 1)
         gather_end(half, False, 2)
     for place in range(11, 15):
         value_block(place)
-    lax.fori_loop(0, 16, weight_block, 0)
     for half in (0, 1):
         gather_end(half, False, 3)
     value_block(15)
     send_part = send(vpart.at[pl.ds(TOK, TOK), :], vrecv, sibling)
-
-    def wrows(half, quarter):
-        return pl.ds(half * 256 + quarter * 128, 128)
-
-    scatter = {}
-
-    def place_of(half, line, by):
-        move = shift(half, by, line) if line < 4 else shift(half, 0, by)
-        return chip_at(*move)
-
-    def scatter_send(half, line, kind, by, quarter, to):
-        scatter[half, line, kind] = send(
-            wt.at[place_of(half, line, by), wrows(half, quarter), :],
-            rbuf.at[half * 5 + line, kind],
-            peer(*step(half, line < 4, to)),
-        )
-
-    def scatter_far(half, line):
-        scatter_send(half, line, 0, 2, 0, 1)
-        scatter_send(half, line, 1, 2, 1, 3)
-
-    def scatter_near(half, line):
-        scatter_send(half, line, 2, 1, 1, 1)
-        scatter_send(half, line, 3, 3, 0, 3)
-
-    def add_in(half, line, by, quarter, kinds):
-        j = place_of(half, line, by)
-        total = wt[j, wrows(half, quarter), :].astype(F32)
-        for kind in kinds:
-            total = total + rbuf[half * 5 + line, kind].astype(F32)
-        return j, total
-
-    def scatter_forward(half, line):
-        for kind, by, quarter in ((0, 1, 0), (1, 3, 1)):
-            scatter[half, line, kind].wait_recv()
-            j, total = add_in(half, line, by, quarter, (kind,))
-            wt[j, wrows(half, quarter), :] = total.astype(BF16)
-            scatter_send(half, line, kind + 4, by, quarter, by)
-
-    def scatter_own(half, line):
-        for kind in (2, 3, 4, 5):
-            scatter[half, line, kind].wait_recv()
-        for quarter, kinds in ((0, (3, 4)), (1, (2, 5))):
-            j, total = add_in(half, line, 0, quarter, kinds)
-            if line < 4:
-                wt[j, wrows(half, quarter), :] = total.astype(BF16)
-            else:
-                fin[wrows(half, quarter), :] = total
-
-    lines = (2, 1, 3, 0)
-    for line in lines:
-        for half in (0, 1):
-            scatter_far(half, line)
-    for line in lines:
-        for half in (0, 1):
-            scatter_near(half, line)
+    pl.when(is_top)(open_scatter)
 
     send_part.wait_recv()
     whole = vpart[0:TOK, :] + vrecv[...]
     values[...] = whole.astype(BF16)
     mean = jnp.sum(whole * vg[0:TOK, :].astype(F32), axis=1, keepdims=True) * (1.0 / D)
     cen[...] = jnp.broadcast_to(mean, (TOK, 128))
-    send_cen1 = remote(cen, cen1, below, "down")
+    cen_row[...] = cen[...].T[0:8, :]
+    send_cen1 = remote(cen_row, cen1_row, below, "down")
 
     for copy in ng_copies:
         copy.wait_recv()
@@ -386,26 +475,42 @@
         lates.append((j, remote(
             stream.at[:, where], late.at[:, pl.ds((e - EARLY) * 512, 512)], below, "down"
         )))
-    outs = [
-        pltpu.make_async_copy(
-            stream.at[:, pl.ds(n * 512, 512)], stream_o.at[:, pl.ds(n * 512, 512)], lsem.at[next(local_ids)]
-        )
-        for n in range(16)
-    ]
-
     def top_block(j):
         where = cols(j * 512, 512)
         stream[:, where] = (top[:, where].astype(F32) + own_branch(where)).astype(BF16)
 
-    @pl.when(is_top)
-    def _():
-        send_cen1.start()
-        for j, copy in lates:
-            top_block(j)
-            copy.start()
-
-    for half in (0, 1):
-        scatter_forward(half, 2)
+    def send_lates(start, stop):
+        @pl.when(is_top)
+        def _():
+            if start == 0:
+                send_cen1.start()
+            for j, copy in lates[start:stop]:
+                top_block(j)
+                copy.start()
+
+        @pl.when(is_low)
+        def _():
+            for n in range(2 * start, 2 * stop):
+                where = pl.ds(n * 512, 512)
+                own[:, where] = own_branch(where)
+
+    def top_early(start, stop):
+        @pl.when(is_top)
+        def _():
+            for j, _, _ in early[start:stop]:
+                top_block(j)
+
+    send_lates(0, 2)
+    scatter_stage(0, 0)
+    scatter_stage(0, 1)
+    scatter_start(1)
+    send_lates(2, 3)
+    scatter_stage(0, 2)
+    scatter_start_near(1)
+    send_lates(3, 4)
+    scatter_stage(0, 3)
+    scatter_stage(1, 0)
+    send_lates(4, 5)
 
     def attend_back(k):
         lanes = slice(k * HEAD, (k + 1) * HEAD)
@@ -421,27 +526,6 @@
             head = (GROUP * k + g) * HEAD
             qg[:, head:head + HEAD] = dot(turned, key[:, lanes]).astype(BF16)
 
-    attend_back(0)
-    for line in (1, 3):
-        for half in (0, 1):
-            scatter_forward(half, line)
-    attend_back(1)
-    for half in (0, 1):
-        scatter_forward(half, 0)
-        scatter_own(half, 2)
-        scatter_far(half, 4)
-    attend_back(2)
-    for half in (0, 1):
-        scatter_own(half, 1)
-        scatter_own(half, 3)
-        scatter_near(half, 4)
-    attend_back(3)
-    out_qg = local(qg, qg_o)
-    out_kg = local(kg, kg_o)
-    for half in (0, 1):
-        scatter_own(half, 0)
-        scatter_forward(half, 4)
-
     ng1_copies = []
     forward_vg1 = remote(vg1.at[pl.ds(0, TOK), :], vg1.at[pl.ds(TOK, TOK), :], sibling, "low")
     for e in range(EARLY):
@@ -452,16 +536,61 @@
     def _():
         send_vg1.wait_recv()
         forward_vg1.start()
-        forward_vg1.wait_recv()
-        for e in range(EARLY):
-            early[e][2].wait_recv()
-            grad = dot_nt(vg1[...], w1[e])
-            ng1[:, cols(e * 512 + core * BLK, BLK)] = grad[0:TOK].astype(BF16)
-            ng1_stage[e] = grad[TOK:].astype(BF16)
-            ng1_copies[e].start()
+
+    def early_grads(start, stop):
+        @pl.when(is_low)
+        def _():
+            if start == 0:
+                forward_vg1.wait_recv()
+            for e in range(start, stop):
+                for half in (0, 1):
+                    early[e][2][half].wait_recv()
+                grad = dot_nt(vg1[...], w1[e])
+                ng1[:, cols(e * 512 + core * BLK, BLK)] = grad[0:TOK].astype(BF16)
+                ng1_stage[e] = grad[TOK:].astype(BF16)
+                ng1_copies[e].start()
+
+    wown[...] = w_all[chip].astype(F32).T
+
+    def finish(wave):
+        for o in (4, 5, 6):
+            rep_copies[wave, o].wait_recv()
+        summed = jnp.concatenate([rep_all[wave, q].astype(F32) for q in range(4)], axis=0) * GRAD_SCALE
+        here = slice(wave * 128, wave * 128 + 128)
+        vwg[here, :] = summed.T
+        gain_own = gain[:, cols(shard * BLK + wave * 128, 128)]
+        gg[:, here] = jnp.sum(summed * wown[:, here], axis=0, keepdims=True) / gain_own
+
+    scatter_stage(0, 4)
+    attend_back(0)
+    send_lates(5, 6)
+    scatter_stage(1, 1)
+    scatter_stage(0, 5)
+    attend_back(1)
+    send_lates(6, 7)
+    scatter_stage(1, 2)
+    scatter_stage(0, 6)
+    early_grads(0, 2)
+    attend_back(2)
+    send_lates(7, 16 - EARLY)
+    scatter_stage(1, 3)
+    early_grads(2, 4)
+    attend_back(3)
+    top_early(0, EARLY // 2)
+    scatter_stage(1, 4)
+    top_early(EARLY // 2, EARLY)
+    scatter_stage(1, 5)
+    early_grads(4, EARLY)
+    finish(0)
+    scatter_stage(1, 6)
+
+    @pl.when(is_low)
+    def _():
         send_inv1.wait_recv()
         send_gain1.wait_recv()
         send_cen1.wait_recv()
+        inv1[...] = jnp.broadcast_to(inv1_row[0:1, :], (TOK, 128)).T
+        cen1[...] = jnp.broadcast_to(cen1_row[0:1, :], (TOK, 128)).T
         for e in range(EARLY):
             ng1_copies[e].wait_recv()
             early[e][1].wait_recv()
@@ -469,52 +598,14 @@
             where = cols(early[e][0] * 512, 512)
             upper = branch(hid1[:, here], inv1, ng1[:, here], gain1[:, where], cen1)
             upper = (top[:, where].astype(F32) + upper).astype(BF16)
-            stream[:, where] = (upper.astype(F32) + own_branch(where)).astype(BF16)
-
-    @pl.when(is_top)
-    def _():
-        for j, _, _ in early:
-            top_block(j)
-
-    for half in (0, 1):
-        scatter_own(half, 4)
-
-    for o in (1, 2, 3):
-        q = lax.rem(rep + o, 4)
-        rep_stage[o] = fin[pl.ds(pl.multiple_of(q * 128, 128), 128), :].astype(BF16)
-    rep_copies = [
-        send(rep_stage.at[o], rep_recv.at[o - 1], {"rep": lax.rem(rep + o, 4)}) for o in (1, 2, 3)
-    ]
-    mine = pl.ds(pl.multiple_of(rep * 128, 128), 128)
-    wown[...] = w_all[chip].astype(F32).T
-    total = fin[mine, :]
-    for o in (1, 2, 3):
-        rep_copies[o - 1].wait_recv()
-        total = total + rep_recv[o - 1].astype(F32)
-    rep_all[rep] = total.astype(BF16)
-    all_copies = [
-        send(rep_all.at[rep], rep_all.at[rep], {"rep": lax.rem(rep + o, 4)}) for o in (1, 2, 3)
-    ]
-
-    @pl.when(is_low)
-    def _():
+            stream[:, where] = (upper.astype(F32) + own[:, where]).astype(BF16)
         for e, (j, copy) in enumerate(lates):
             copy.wait_recv()
             where = cols(j * 512, 512)
             upper = late[:, pl.ds(e * 512, 512)].astype(F32)
-            stream[:, where] = (upper + own_branch(where)).astype(BF16)
-
-    for copy in outs:
-        copy.start()
-    for copy in all_copies:
-        copy.wait_recv()
-    summed = jnp.concatenate([rep_all[q].astype(F32) for q in range(4)], axis=0) * GRAD_SCALE
-    vwg[...] = summed.T
-    gain_own = gain[:, cols(shard * BLK, BLK)]
-    gg[...] = jnp.sum(summed * wown[...], axis=0, keepdims=True) / gain_own
-    ends = [local(vwg, vwg_o), local(gg, gg_o), out_qg, out_kg] + outs
-    for copy in ends:
-        copy.wait()
+            stream[:, where] = (upper + own[:, where]).astype(BF16)
+
+    finish(1)
 
     for copy, who in sent:
         if who is None:
@@ -533,6 +624,15 @@
                 copy.wait_send()
 
 
+def store_kernel(*refs):
+    parts, outs, sems = refs[:5], refs[5:10], refs[10]
+    copies = [pltpu.make_async_copy(parts[n], outs[n], sems.at[n]) for n in range(5)]
+    for copy in copies:
+        copy.start()
+    for copy in copies:
+        copy.wait()
+
+
 def per_device(hidden_in, query_rows, key_rows, context_grad, stream_top, norm_gain, value_weight):
     def vmem(*shape, dtype=BF16):
         return pltpu.VMEM(shape, dtype)
@@ -540,35 +640,38 @@
     scratch = [
         vmem(TOK, D), vmem(TOK, D // 2), vmem(TOK, 4096), vmem(TOK, KVW), vmem(TOK, 4096), vmem(TOK, D),
         vmem(1, D, dtype=F32), vmem(1, D, dtype=F32),
-        *[vmem(TOK, 128, dtype=F32) for _ in range(5)],
+        *[vmem(TOK, 128, dtype=F32) for _ in range(5)], *[vmem(8, 128, dtype=F32) for _ in range(4)],
         vmem(16, BLK, KVW), vmem(EARLY, BLK, KVW), vmem(2 * TOK, 4096),
         vmem(2 * TOK, KVW), vmem(2 * TOK, KVW), vmem(KVW, 2 * TOK),
         vmem(KV, TOK, GROUP * TOK, dtype=F32),
         vmem(2 * TOK, KVW, dtype=F32), vmem(TOK, KVW, dtype=F32), vmem(TOK, KVW),
         vmem(TOK, D), vmem(16, TOK, BLK), vmem(TOK, EARLY * 512), vmem(EARLY, TOK, BLK),
-        vmem(TOK, EARLY * 512), vmem(TOK, D), vmem(TOK, (16 - EARLY) * 512),
-        vmem(16, KVW, BLK), vmem(10, 6, 128, BLK), vmem(KVW, BLK, dtype=F32),
-        vmem(4, 128, BLK), vmem(3, 128, BLK), vmem(4, 128, BLK), vmem(KVW, BLK, dtype=F32),
-        vmem(TOK, 4096), vmem(TOK, KVW), vmem(BLK, KVW, dtype=F32), vmem(1, BLK, dtype=F32),
+        vmem(TOK, EARLY * 512), vmem(TOK, (16 - EARLY) * 512), vmem(TOK, D, dtype=F32),
+        vmem(16, KVW, BLK), vmem(20, 6, 128, 128), vmem(2, 4, 128, 128, dtype=F32),
+        vmem(2, 4, 128, 128), vmem(2, 3, 128, 128), vmem(2, 4, 128, 128), vmem(KVW, BLK, dtype=F32),
         pltpu.SemaphoreType.DMA((NSEM,)), pltpu.SemaphoreType.DMA((NSEM,)), pltpu.SemaphoreType.DMA((32,)),
     ]
-    outs = pl.pallas_call(
+    out_shapes = (((TOK, D), BF16), ((TOK, 4096), BF16), ((TOK, KVW), BF16), ((BLK, KVW), F32), ((1, BLK), F32))
+    args = hidden_in[0], query_rows[0], key_rows[0], context_grad[0], stream_top, norm_gain, value_weight[0]
+    parts = pl.pallas_call(
         kernel,
-        out_shape=(
-            jax.ShapeDtypeStruct((TOK, D), BF16),
-            jax.ShapeDtypeStruct((TOK, 4096), BF16),
-            jax.ShapeDtypeStruct((TOK, KVW), BF16),
-            jax.ShapeDtypeStruct((BLK, KVW), F32),
-            jax.ShapeDtypeStruct((1, BLK), F32),
-        ),
+        out_shape=tuple(pltpu.VMEM(*shape) for shape in out_shapes),
         in_specs=[pl.BlockSpec(memory_space=pl.ANY)] * 7,
-        out_specs=[pl.BlockSpec(memory_space=pl.ANY)] * 5,
+        out_specs=[pl.BlockSpec(memory_space=pltpu.VMEM)] * 5,
         scratch_shapes=scratch,
         compiler_params=pltpu.CompilerParams(
-            collective_id=0, has_side_effects=True, vmem_limit_bytes=56 * 1024 * 1024
+            collective_id=0, has_side_effects=True, vmem_limit_bytes=48 * 1024 * 1024
         ),
         cost_estimate=pl.CostEstimate(flops=5 * 10**9, bytes_accessed=12 * 10**6, transcendentals=10**6),
-    )(hidden_in[0], query_rows[0], key_rows[0], context_grad[0], stream_top, norm_gain, value_weight[0])
+    )(*[pltpu.with_memory_space_constraint(arg, pltpu.HBM) for arg in args])
+    outs = pl.pallas_call(
+        store_kernel,
+        out_shape=tuple(jax.ShapeDtypeStruct(*shape) for shape in out_shapes),
+        in_specs=[pl.BlockSpec(memory_space=pltpu.VMEM)] * 5,
+        out_specs=[pl.BlockSpec(memory_space=pl.ANY)] * 5,
+        scratch_shapes=[pltpu.SemaphoreType.DMA((5,))],
+        compiler_params=pltpu.CompilerParams(vmem_limit_bytes=1024 * 1024),
+    )(*[pltpu.with_memory_space_constraint(part, pltpu.VMEM) for part in parts])
     stream, query_grad, key_grad, weight_grad, gain_grad = outs
     return stream[None], query_grad[None], key_grad[None], weight_grad[None], gain_grad
 

time: 93.5 us -> 87.5 us (0.936)
  local copies, waits for them, and re-layouts: 6.2 us -> 0 us
    unnamed x13 -> x0, local copies, waits for them, and re-layouts: 6.2 us -> none
    pallas_call x1 -> x2, Pallas kernels: 85.9 us -> 86.7 us  [the longest x1 84.7 us: per_device(): pl.pallas_call(kernel, out_shape=tuple((pltpu.VMEM(*shape) for shape in o...]
where the time goes in v2:
time: 87.5 us
  Pallas kernels  86.7 us (99%)
    pallas_call x1, Pallas kernels, per_device(): pl.pallas_call(kernel, out_shape=tuple((pltpu.VMEM(*shape) for shape in o...  84.7 us
    pallas_call x1, Pallas kernels, per_device(): pl.pallas_call(store_kernel, out_shape=tuple((jax.ShapeDtypeStruct(*shape...  1.92 us

profile of v2, /device:TPU:32, one launch (start us, length us, event | category | flops | bytes accessed | tf_op | source)
XLA Modules:
  0.0 87.5 jit_solution(11503065981722776897)
XLA Ops:
  0.6 84.7 %shard_map.110 = (bf16[128,8192]{1,0:T(8,128)(2,1)S(1)}, bf16[128,4096]{1,0:T(8,128)(2,1)S(1)}, bf16[128,512]{1,0:T(8,128)(2,1)S(1)}, f32[256,512]{1,0:T(8,128)S(1)}, f32[1,256]{1,0:T(1,128)S(1)}) custom-call(bf16[128,8192]{1,0:T(8,128)(2,1)} %bitcast.9, bf16[128,4096]{1,0:T(8,128)(2,1)} %bitcast.11, bf16[128,512]{1,0:T(8,128)(2,1)} %bitcast.16, ...), custom_call_target="tpu_custom_call" | custom-call | flops 5000000000 | bytes 12000000 | tf_op jit(solution)/shard_map/pallas_call | solution.py:656
  85.4 1.9 %shard_map.111 = (bf16[128,8192]{1,0:T(8,128)(2,1)}, bf16[128,4096]{1,0:T(8,128)(2,1)}, bf16[128,512]{1,0:T(8,128)(2,1)}, f32[256,512]{1,0:T(8,128)}, f32[1,256]{1,0:T(1,128)}) custom-call(bf16[128,8192]{1,0:T(8,128)(2,1)S(1)} %get-tuple-element.15.refs_0_, bf16[128,4096]{1,0:T(8,128)(2,1)S(1)} %get-tuple-element.16.refs_1_, ...), custom_call_target="tpu_custom_call" | custom-call | tf_op jit(solution)/shard_map/pallas_call | solution.py:667

commit v3 on v2

--- a/solution.py
+++ b/solution.py
@@ -25,7 +25,7 @@
     (3, 3), (1, 3), (3, 1), (1, 1), (2, 3), (2, 1), (3, 2), (1, 2), (2, 2),
 )
 EARLY = 8
-NSEM = 228 + 3 * EARLY
+NSEM = 164 + 3 * EARLY
 
 
 def dot(a, b):
@@ -43,7 +43,7 @@
     inv_row, inv1_row, cen_row, cen1_row,
     w_all, w1, normed, vg, vg1, vgt, probs, vpart, vrecv, values,
     ng, ng_stage, ng1, ng1_stage, hid1, late, own,
-    wt, rbuf, fin, rep_stage, rep_recv, rep_all, wown,
+    wt, rfirst, rlast, fin, rep_stage, rep_recv, rep_all, wown,
     ssem, rsem, lsem,
 ):
     pipe = lax.axis_index("pipe")
@@ -90,6 +90,12 @@
     def cols(start, width):
         return pl.ds(pl.multiple_of(start, 128), width)
 
+    barrier = pltpu.get_barrier_semaphore()
+    partners = [peer(1, 0), peer(3, 0), peer(0, 1), peer(0, 3), sibling, {"pipe": 1 - pipe}]
+    partners += [{"rep": lax.rem(rep + o, 4)} for o in (1, 3)]
+    partners += [{"pipe": 1 - pipe, "rep": lax.rem(rep + jnp.where(is_top, 1, 3), 4)}]
+    for device in partners:
+        pl.semaphore_signal(barrier, inc=1, device_id=device, device_id_type=pl.DeviceIdType.MESH)
     load_hid = local(hid_h, hid)
     load_gain = local(gain_h, gain)
     load_key = local(key_h, key)
@@ -98,12 +104,6 @@
     load_w = local(w_h, w_all.at[chip])
     load_top = local(top_h, top)
 
-    barrier = pltpu.get_barrier_semaphore()
-    partners = [peer(1, 0), peer(3, 0), peer(0, 1), peer(0, 3), sibling, {"pipe": 1 - pipe}]
-    partners += [{"rep": lax.rem(rep + o, 4)} for o in (1, 2, 3)]
-    partners += [{"pipe": 1 - pipe, "rep": lax.rem(rep + jnp.where(is_top, 1, 3), 4)}]
-    for device in partners:
-        pl.semaphore_signal(barrier, inc=1, device_id=device, device_id_type=pl.DeviceIdType.MESH)
     pl.semaphore_wait(barrier, len(partners))
 
     def step(half, first, by):
@@ -217,31 +217,20 @@
         probs[k] = prob
         vg[0:TOK, lanes] = dot(prob.astype(BF16), stacked(ctx, k)).astype(BF16)
 
+    def top_blocks_ahead(pairs):
+        @pl.when(is_top)
+        def _():
+            for e, half in pairs:
+                early[e][2][half].start()
+
     attend(0)
+    attend(1)
     for half in (0, 1):
         gather_forward(half, True, 0, 0)
         gather_pass(half, 3, 1)
         gather_pass(half, 1, 2)
-
-    @pl.when(is_top)
-    def _():
-        for e, half in ((1, 0), (2, 0), (3, 1), (4, 1)):
-            early[e][2][half].start()
-
-    attend(1)
-    for half in (0, 1):
-        gather_forward(half, False, 0, 0)
-    load_w.wait()
-
-    @pl.when(is_top)
-    def _():
-        for e, half in ((1, 1), (2, 1), (3, 0), (4, 0)):
-            early[e][2][half].start()
-
+    top_blocks_ahead(((1, 0), (2, 0), (3, 1), (4, 1)))
     attend(2)
-    for half in (0, 1):
-        gather_end(half, True, 0)
-        gather_pass(half, 2, 3)
     attend(3)
 
     send_vg = send(vg.at[pl.ds(0, TOK), :], vg.at[pl.ds(TOK, TOK), :], sibling)
@@ -252,13 +241,9 @@
         send_vg1.start()
 
     for half in (0, 1):
-        gather_end(half, False, 0)
-
-    @pl.when(is_top)
-    def _():
-        for e in range(5, 7):
-            for half in (0, 1):
-                early[e][2][half].start()
+        gather_forward(half, False, 0, 0)
+    load_w.wait()
+    top_blocks_ahead(((1, 1), (2, 1), (3, 0), (4, 0)))
 
     for copy in hsib_copies:
         copy.wait_recv()
@@ -266,170 +251,174 @@
 
     def norm_block(j, carry):
         gain_row = gain[:, cols((2 * j + core) * BLK, BLK)]
-        own = hid[:, cols((2 * j + core) * BLK, BLK)].astype(F32) * inv[:, 0:1]
+        mine = hid[:, cols((2 * j + core) * BLK, BLK)].astype(F32) * inv[:, 0:1]
         other = hsib[:, cols(j * BLK, BLK)].astype(F32) * inv_sib[:, 0:1]
-        normed[0:TOK, cols(j * BLK, BLK)] = (own * gain_row).astype(BF16)
+        normed[0:TOK, cols(j * BLK, BLK)] = (mine * gain_row).astype(BF16)
         normed[TOK:, cols(j * BLK, BLK)] = (other * gain_row).astype(BF16)
         return carry
 
     lax.fori_loop(0, 16, norm_block, 0)
     for half in (0, 1):
+        gather_end(half, True, 0)
+        gather_pass(half, 2, 3)
+
+    send_vg.wait_recv()
+    vgt[...] = vg[...].astype(F32).T.astype(BF16)
+
+    def weight_block(place, carry):
+        dx, dy = lax.div(place, 4), lax.rem(place, 4)
+        j = lax.rem(y + dy, 4) * 4 + lax.rem(x + dx, 4)
+        wt[dx, dy] = dot(vgt[...], normed[:, cols(j * BLK, BLK)]).astype(BF16)
+        return carry
+
+    lax.fori_loop(0, 8, weight_block, 0)
+    for half in (0, 1):
+        gather_end(half, False, 0)
+    top_blocks_ahead(((5, 0), (5, 1), (6, 0), (6, 1)))
+    for half in (0, 1):
         gather_forward(half, False, 1, 3)
         gather_forward(half, False, 2, 1)
-
-    send_vg.wait_recv()
-    vgt[...] = vg[...].astype(F32).T.astype(BF16)
-
-    def weight_block(j, carry):
-        wt[j] = dot(vgt[...], normed[:, cols(j * BLK, BLK)]).astype(BF16)
-        return carry
-
-    ng_copies = []
+    top_blocks_ahead(tuple((e, half) for e in range(7, EARLY) for half in (0, 1)))
+    lax.fori_loop(8, 16, weight_block, 0)
 
     def value_block(place):
         j = chip_at(*ORDER[place])
-        block = w_all[j]
-        part = dot(normed[:, cols(j * BLK, BLK)], block)
+        part = dot(normed[:, cols(j * BLK, BLK)], w_all[j])
         if place == 0:
             vpart[...] = part
         else:
             vpart[...] += part
-        grad = dot_nt(vg[...], block)
+
+    ng_copies = {}
+    ng_waited = set()
+
+    def grad_block(place):
+        j = chip_at(*ORDER[place])
+        grad = dot_nt(vg[...], w_all[j])
         where = cols((2 * j + core) * BLK, BLK)
         ng[:, where] = grad[0:TOK].astype(BF16)
         ng_stage[place] = grad[TOK:].astype(BF16)
-        ng_copies.append(send(ng_stage.at[place], ng.at[:, where], sibling))
-
-    @pl.when(is_top)
-    def _():
-        for e in range(7, EARLY):
-            for half in (0, 1):
-                early[e][2][half].start()
+        ng_copies[place] = send(ng_stage.at[place], ng.at[:, where], sibling)
+
+    def grads_ready(start, stop):
+        for place in range(start, stop):
+            if place not in ng_waited:
+                ng_waited.add(place)
+                ng_copies[place].wait_recv()
 
     def wrows(half, quarter):
         return pl.ds(half * 256 + quarter * 128, 128)
 
     scatter = {}
 
-    def place_of(half, line, by):
-        move = shift(half, by, line) if line < 4 else shift(half, 0, by)
-        return chip_at(*move)
-
     def lanes_of(wave):
         return pl.ds(wave * 128, 128)
 
-    def scatter_make(wave, half, line, kind, by, quarter, to):
-        scatter[wave, half, line, kind] = remote(
-            wt.at[place_of(half, line, by), wrows(half, quarter), lanes_of(wave)],
-            rbuf.at[wave * 10 + half * 5 + line, kind],
-            peer(*step(half, line < 4, to)),
+    def term(wave, half, first, by, quarter):
+        along, across = (by, slice(None)) if first else (0, by)
+        place = (along, across) if half == 0 else (across, along)
+        return wt.at[place[0], place[1], wrows(half, quarter), lanes_of(wave)]
+
+    def landing(wave, half, first, kind):
+        return (rfirst if first else rlast).at[wave, half, kind]
+
+    def scatter_make(wave, half, first, kind, by, quarter, to):
+        scatter[wave, half, first, kind] = remote(
+            term(wave, half, first, by, quarter),
+            landing(wave, half, first, kind),
+            peer(*step(half, first, to)),
         )
-        return scatter[wave, half, line, kind]
-
-    def scatter_send(*what):
-        scatter_make(*what).start()
-
-    def scatter_far(wave, line):
-        for half in (0, 1):
-            scatter_send(wave, half, line, 0, 2, 0, 1)
-            scatter_send(wave, half, line, 1, 2, 1, 3)
-
-    def scatter_near(wave, line):
-        for half in (0, 1):
-            scatter_send(wave, half, line, 2, 1, 1, 1)
-            scatter_send(wave, half, line, 3, 3, 0, 3)
-
-    def add_in(wave, half, line, by, quarter, kinds):
-        j = place_of(half, line, by)
-        total = wt[j, wrows(half, quarter), lanes_of(wave)].astype(F32)
+        return scatter[wave, half, first, kind]
+
+    def scatter_open(wave, first):
+        copies = []
+        for kind, by, quarter, to in ((0, 2, 0, 1), (1, 2, 1, 3), (2, 1, 1, 1), (3, 3, 0, 3)):
+            for half in (0, 1):
+                copies.append(scatter_make(wave, half, first, kind, by, quarter, to))
+        return copies
+
+    def add_in(wave, half, first, by, quarter, kinds):
+        total = term(wave, half, first, by, quarter)[...].astype(F32)
         for kind in kinds:
-            total = total + rbuf[wave * 10 + half * 5 + line, kind].astype(F32)
-        return j, total
-
-    def scatter_forward(wave, line):
+            total = total + landing(wave, half, first, kind)[...].astype(F32)
+        return total
+
+    def scatter_forward(wave, first):
         for half in (0, 1):
             for kind, by, quarter in ((0, 1, 0), (1, 3, 1)):
-                scatter[wave, half, line, kind].wait_recv()
-                j, total = add_in(wave, half, line, by, quarter, (kind,))
-                wt[j, wrows(half, quarter), lanes_of(wave)] = total.astype(BF16)
-                scatter_send(wave, half, line, kind + 4, by, quarter, by)
-
-    def scatter_own(wave, line):
+                scatter[wave, half, first, kind].wait_recv()
+                total = add_in(wave, half, first, by, quarter, (kind,))
+                term(wave, half, first, by, quarter)[...] = total.astype(BF16)
+                scatter_make(wave, half, first, kind + 4, by, quarter, by).start()
+
+    def scatter_own(wave, first):
         for half in (0, 1):
             for kind in (2, 3, 4, 5):
-                scatter[wave, half, line, kind].wait_recv()
+                scatter[wave, half, first, kind].wait_recv()
             for quarter, kinds in ((0, (3, 4)), (1, (2, 5))):
-                j, total = add_in(wave, half, line, 0, quarter, kinds)
-                if line < 4:
-                    wt[j, wrows(half, quarter), lanes_of(wave)] = total.astype(BF16)
+                total = add_in(wave, half, first, 0, quarter, kinds)
+                if first:
+                    term(wave, half, first, 0, quarter)[...] = total.astype(BF16)
                 else:
                     fin[wave, half * 2 + quarter] = total
 
+    after, before, across = lax.rem(rep + 1, 4), lax.rem(rep + 3, 4), lax.rem(rep + 2, 4)
+    halves = (slice(0, 64), slice(64, 128))
     rep_copies = {}
 
-    def rep_first(wave):
-        for o in (1, 2, 3):
-            q = lax.rem(rep + o, 4)
-            rep_stage[wave, o] = fin[wave, q].astype(BF16)
-            rep_copies[wave, o] = send(rep_stage.at[wave, o], rep_recv.at[wave, o - 1], {"rep": q})
-
-    def rep_second(wave):
-        total = fin[wave, rep]
-        for o in (1, 2, 3):
-            rep_copies[wave, o].wait_recv()
-            total = total + rep_recv[wave, o - 1].astype(F32)
-        rep_all[wave, rep] = total.astype(BF16)
-        for o in (1, 2, 3):
-            here = rep_all.at[wave, rep]
-            rep_copies[wave, o + 3] = send(here, here, {"rep": lax.rem(rep + o, 4)})
-
-    def scatter_start(wave):
-        for line in (2, 1, 3, 0):
-            scatter_far(wave, line)
-
-    def scatter_start_near(wave):
-        for line in (2, 1, 3, 0):
-            scatter_near(wave, line)
+    def rep_send(wave, kind, value, to):
+        rep_stage[wave, kind] = value.astype(BF16)
+        rep_copies[wave, kind] = send(rep_stage.at[wave, kind], rep_recv.at[wave, kind], {"rep": to})
+
+    def rep_got(wave, kind):
+        rep_copies[wave, kind].wait_recv()
+        return rep_recv[wave, kind].astype(F32)
+
+    def rep_stage_of(wave, stage):
+        if stage == 0:
+            rep_send(wave, 0, fin[wave, across, halves[0], :], after)
+            rep_send(wave, 1, fin[wave, across, halves[1], :], before)
+            rep_send(wave, 2, fin[wave, after, halves[1], :], after)
+            rep_send(wave, 3, fin[wave, before, halves[0], :], before)
+        elif stage == 1:
+            rep_send(wave, 4, fin[wave, after, halves[0], :] + rep_got(wave, 0), after)
+            rep_send(wave, 5, fin[wave, before, halves[1], :] + rep_got(wave, 1), before)
+        elif stage == 2:
+            for half, kinds in ((0, (3, 4)), (1, (2, 5))):
+                total = fin[wave, rep, halves[half], :]
+                for kind in kinds:
+                    total = total + rep_got(wave, kind)
+                rep_all[wave, rep, halves[half], :] = total.astype(BF16)
+            for kind, to in ((6, after), (7, before)):
+                here = rep_all.at[wave, rep]
+                rep_copies[wave, kind] = send(here, here, {"rep": to})
+        elif stage == 3:
+            for kind, part, half, to in ((6, before, 0, after), (7, after, 1, before)):
+                rep_copies[wave, kind].wait_recv()
+                here = rep_all.at[wave, part, pl.ds(64 * half, 64), :]
+                rep_copies[wave, kind + 2] = send(here, here, {"rep": to})
+        else:
+            for kind in (8, 9):
+                rep_copies[wave, kind].wait_recv()
 
     def scatter_stage(wave, stage):
         if stage == 0:
-            scatter_forward(wave, 2)
+            scatter_forward(wave, True)
         elif stage == 1:
-            scatter_forward(wave, 1)
-            scatter_forward(wave, 3)
+            scatter_own(wave, True)
+            for copy in scatter_open(wave, False):
+                copy.start()
         elif stage == 2:
-            scatter_forward(wave, 0)
-            scatter_own(wave, 2)
-            scatter_far(wave, 4)
+            scatter_forward(wave, False)
         elif stage == 3:
-            scatter_own(wave, 1)
-            scatter_own(wave, 3)
-            scatter_near(wave, 4)
-        elif stage == 4:
-            scatter_own(wave, 0)
-            scatter_forward(wave, 4)
-        elif stage == 5:
-            scatter_own(wave, 4)
-            rep_first(wave)
-        else:
-            rep_second(wave)
-
-    opening = []
-    for line in (2, 1, 3, 0):
-        for half in (0, 1):
-            opening.append(scatter_make(0, half, line, 0, 2, 0, 1))
-            opening.append(scatter_make(0, half, line, 1, 2, 1, 3))
-    for line in (2, 1, 3, 0):
-        for half in (0, 1):
-            opening.append(scatter_make(0, half, line, 2, 1, 1, 1))
-            opening.append(scatter_make(0, half, line, 3, 3, 0, 3))
+            scatter_own(wave, False)
+            rep_stage_of(wave, 0)
+
+    opening = scatter_open(0, True) + scatter_open(1, True)
 
     def open_scatter():
-        lax.fori_loop(0, 16, weight_block, 0)
         for copy in opening:
             copy.start()
-
-    pl.when(is_low)(open_scatter)
 
     for place in range(0, 7):
         value_block(place)
@@ -444,9 +433,11 @@
         value_block(place)
     for half in (0, 1):
         gather_end(half, False, 3)
+    open_scatter()
     value_block(15)
     send_part = send(vpart.at[pl.ds(TOK, TOK), :], vrecv, sibling)
-    pl.when(is_top)(open_scatter)
+    for place in range(EARLY, EARLY + 4):
+        grad_block(place)
 
     send_part.wait_recv()
     whole = vpart[0:TOK, :] + vrecv[...]
@@ -456,8 +447,6 @@
     cen_row[...] = cen[...].T[0:8, :]
     send_cen1 = remote(cen_row, cen1_row, below, "down")
 
-    for copy in ng_copies:
-        copy.wait_recv()
     load_top.wait()
 
     def branch(hidden, scale, grad, gain_row, center):
@@ -479,7 +468,17 @@
         where = cols(j * 512, 512)
         stream[:, where] = (top[:, where].astype(F32) + own_branch(where)).astype(BF16)
 
+    def own_blocks(start, stop):
+        @pl.when(is_low)
+        def _():
+            for place in range(start, stop):
+                where = cols(chip_at(*ORDER[place]) * 512, 512)
+                own[:, where] = own_branch(where)
+
     def send_lates(start, stop):
+        grads_ready(EARLY + start, EARLY + stop)
+        own_blocks(EARLY + start, EARLY + stop)
+
         @pl.when(is_top)
         def _():
             if start == 0:
@@ -488,13 +487,10 @@
                 top_block(j)
                 copy.start()
 
-        @pl.when(is_low)
-        def _():
-            for n in range(2 * start, 2 * stop):
-                where = pl.ds(n * 512, 512)
-                own[:, where] = own_branch(where)
-
     def top_early(start, stop):
+        grads_ready(start, stop)
+        own_blocks(start, stop)
+
         @pl.when(is_top)
         def _():
             for j, _, _ in early[start:stop]:
@@ -502,15 +498,15 @@
 
     send_lates(0, 2)
     scatter_stage(0, 0)
+    for place in range(EARLY + 4, 16):
+        grad_block(place)
+    send_lates(2, 4)
+    scatter_stage(1, 0)
+    send_lates(4, 6)
+    for place in range(0, EARLY):
+        grad_block(place)
     scatter_stage(0, 1)
-    scatter_start(1)
-    send_lates(2, 3)
-    scatter_stage(0, 2)
-    scatter_start_near(1)
-    send_lates(3, 4)
-    scatter_stage(0, 3)
-    scatter_stage(1, 0)
-    send_lates(4, 5)
+    send_lates(6, 16 - EARLY)
 
     def attend_back(k):
         lanes = slice(k * HEAD, (k + 1) * HEAD)
@@ -553,36 +549,33 @@
     wown[...] = w_all[chip].astype(F32).T
 
     def finish(wave):
-        for o in (4, 5, 6):
-            rep_copies[wave, o].wait_recv()
+        rep_stage_of(wave, 4)
         summed = jnp.concatenate([rep_all[wave, q].astype(F32) for q in range(4)], axis=0) * GRAD_SCALE
         here = slice(wave * 128, wave * 128 + 128)
         vwg[here, :] = summed.T
         gain_own = gain[:, cols(shard * BLK + wave * 128, 128)]
         gg[:, here] = jnp.sum(summed * wown[:, here], axis=0, keepdims=True) / gain_own
 
-    scatter_stage(0, 4)
+    scatter_stage(0, 2)
     attend_back(0)
-    send_lates(5, 6)
     scatter_stage(1, 1)
-    scatter_stage(0, 5)
+    scatter_stage(0, 3)
+    scatter_stage(1, 2)
     attend_back(1)
-    send_lates(6, 7)
-    scatter_stage(1, 2)
-    scatter_stage(0, 6)
+    rep_stage_of(0, 1)
+    scatter_stage(1, 3)
+    attend_back(2)
+    rep_stage_of(0, 2)
+    rep_stage_of(1, 1)
+    attend_back(3)
     early_grads(0, 2)
-    attend_back(2)
-    send_lates(7, 16 - EARLY)
-    scatter_stage(1, 3)
-    early_grads(2, 4)
-    attend_back(3)
-    top_early(0, EARLY // 2)
-    scatter_stage(1, 4)
-    top_early(EARLY // 2, EARLY)
-    scatter_stage(1, 5)
-    early_grads(4, EARLY)
+    rep_stage_of(0, 3)
+    rep_stage_of(1, 2)
+    early_grads(2, EARLY)
+    top_early(0, 4)
+    rep_stage_of(1, 3)
+    top_early(4, EARLY)
     finish(0)
-    scatter_stage(1, 6)
 
     @pl.when(is_low)
     def _():
@@ -647,8 +640,8 @@
         vmem(2 * TOK, KVW, dtype=F32), vmem(TOK, KVW, dtype=F32), vmem(TOK, KVW),
         vmem(TOK, D), vmem(16, TOK, BLK), vmem(TOK, EARLY * 512), vmem(EARLY, TOK, BLK),
         vmem(TOK, EARLY * 512), vmem(TOK, (16 - EARLY) * 512), vmem(TOK, D, dtype=F32),
-        vmem(16, KVW, BLK), vmem(20, 6, 128, 128), vmem(2, 4, 128, 128, dtype=F32),
-        vmem(2, 4, 128, 128), vmem(2, 3, 128, 128), vmem(2, 4, 128, 128), vmem(KVW, BLK, dtype=F32),
+        vmem(4, 4, KVW, BLK), vmem(2, 2, 6, 4, 128, 128), vmem(2, 2, 6, 128, 128), vmem(2, 4, 128, 128, dtype=F32),
+        vmem(2, 6, 64, 128), vmem(2, 6, 64, 128), vmem(2, 4, 128, 128), vmem(KVW, BLK, dtype=F32),
         pltpu.SemaphoreType.DMA((NSEM,)), pltpu.SemaphoreType.DMA((NSEM,)), pltpu.SemaphoreType.DMA((32,)),
     ]
     out_shapes = (((TOK, D), BF16), ((TOK, 4096), BF16), ((TOK, KVW), BF16), ((BLK, KVW), F32), ((1, BLK), F32))

time: 87.5 us -> 84.3 us (0.963)
  Pallas kernels: 86.7 us -> 83.4 us
    pallas_call x1, Pallas kernels: 84.7 us -> 81.5 us  [per_device(): pl.pallas_call(kernel, out_shape=tuple((pltpu.VMEM(*shape) for shape in o...]
where the time goes in v3:
time: 84.3 us; the launch traced here: 84.2 us
  Pallas kernels  83.4 us (99%)
    pallas_call x1, Pallas kernels, per_device(): pl.pallas_call(kernel, out_shape=tuple((pltpu.VMEM(*shape) for shape in o...  81.5 us
    pallas_call x1, Pallas kernels, per_device(): pl.pallas_call(store_kernel, out_shape=tuple((jax.ShapeDtypeStruct(*shape...  1.92 us

profile of v3, /device:TPU:32, one launch (start us, length us, event | category | flops | bytes accessed | tf_op | source)
XLA Modules:
  0.0 84.2 jit_solution(15491107292943949201)
XLA Ops:
  0.6 81.5 %shard_map.110 = (bf16[128,8192]{1,0:T(8,128)(2,1)S(1)}, bf16[128,4096]{1,0:T(8,128)(2,1)S(1)}, bf16[128,512]{1,0:T(8,128)(2,1)S(1)}, f32[256,512]{1,0:T(8,128)S(1)}, f32[1,256]{1,0:T(1,128)S(1)}) custom-call(bf16[128,8192]{1,0:T(8,128)(2,1)} %bitcast.9, bf16[128,4096]{1,0:T(8,128)(2,1)} %bitcast.11, bf16[128,512]{1,0:T(8,128)(2,1)} %bitcast.16, ...), custom_call_target="tpu_custom_call" | custom-call | flops 5000000000 | bytes 12000000 | tf_op jit(solution)/shard_map/pallas_call | solution.py:649
  82.2 1.9 %shard_map.111 = (bf16[128,8192]{1,0:T(8,128)(2,1)}, bf16[128,4096]{1,0:T(8,128)(2,1)}, bf16[128,512]{1,0:T(8,128)(2,1)}, f32[256,512]{1,0:T(8,128)}, f32[1,256]{1,0:T(1,128)}) custom-call(bf16[128,8192]{1,0:T(8,128)(2,1)S(1)} %get-tuple-element.15.refs_0_, bf16[128,4096]{1,0:T(8,128)(2,1)S(1)} %get-tuple-element.16.refs_1_, ...), custom_call_target="tpu_custom_call" | custom-call | tf_op jit(solution)/shard_map/pallas_call | solution.py:660

commit v4 on v3

--- a/solution.py
+++ b/solution.py
@@ -424,6 +424,7 @@
         value_block(place)
     for half in (0, 1):
         gather_forward(half, False, 3, 2)
+    pl.when(is_low)(open_scatter)
     for place in range(7, 11):
         value_block(place)
     for half in (0, 1):
@@ -433,7 +434,7 @@
         value_block(place)
     for half in (0, 1):
         gather_end(half, False, 3)
-    open_scatter()
+    pl.when(is_top)(open_scatter)
     value_block(15)
     send_part = send(vpart.at[pl.ds(TOK, TOK), :], vrecv, sibling)
     for place in range(EARLY, EARLY + 4):
@@ -503,10 +504,10 @@
     send_lates(2, 4)
     scatter_stage(1, 0)
     send_lates(4, 6)
+    scatter_stage(0, 1)
+    send_lates(6, 16 - EARLY)
     for place in range(0, EARLY):
         grad_block(place)
-    scatter_stage(0, 1)
-    send_lates(6, 16 - EARLY)
 
     def attend_back(k):
         lanes = slice(k * HEAD, (k + 1) * HEAD)

time: 84.3 us -> 85.3 us (1.012); the launches traced: 84.2 us -> 84.2 us
  no operation moved by 1% of the time
where the time goes in v4:
time: 85.3 us; the launch traced here: 84.2 us
  Pallas kernels  83.4 us (98%)
    pallas_call x1, Pallas kernels, per_device(): pl.pallas_call(kernel, out_shape=tuple((pltpu.VMEM(*shape) for shape in o...  81.5 us
    pallas_call x1, Pallas kernels, per_device(): pl.pallas_call(store_kernel, out_shape=tuple((jax.ShapeDtypeStruct(*shape...  1.92 us

profile of v4, /device:TPU:32, one launch (start us, length us, event | category | flops | bytes accessed | tf_op | source)
XLA Modules:
  0.0 84.2 jit_solution(5052858808489267614)
XLA Ops:
  0.6 81.5 %shard_map.110 = (bf16[128,8192]{1,0:T(8,128)(2,1)S(1)}, bf16[128,4096]{1,0:T(8,128)(2,1)S(1)}, bf16[128,512]{1,0:T(8,128)(2,1)S(1)}, f32[256,512]{1,0:T(8,128)S(1)}, f32[1,256]{1,0:T(1,128)S(1)}) custom-call(bf16[128,8192]{1,0:T(8,128)(2,1)} %bitcast.9, bf16[128,4096]{1,0:T(8,128)(2,1)} %bitcast.11, bf16[128,512]{1,0:T(8,128)(2,1)} %bitcast.16, ...), custom_call_target="tpu_custom_call" | custom-call | flops 5000000000 | bytes 12000000 | tf_op jit(solution)/shard_map/pallas_call | solution.py:650
  82.1 1.9 %shard_map.111 = (bf16[128,8192]{1,0:T(8,128)(2,1)}, bf16[128,4096]{1,0:T(8,128)(2,1)}, bf16[128,512]{1,0:T(8,128)(2,1)}, f32[256,512]{1,0:T(8,128)}, f32[1,256]{1,0:T(1,128)}) custom-call(bf16[128,8192]{1,0:T(8,128)(2,1)S(1)} %get-tuple-element.15.refs_0_, bf16[128,4096]{1,0:T(8,128)(2,1)S(1)} %get-tuple-element.16.refs_1_, ...), custom_call_target="tpu_custom_call" | custom-call | tf_op jit(solution)/shard_map/pallas_call | solution.py:661
